TPU v7x, 32 devices: a whole 2x2x4 slice. The times are simulated.
32 devices in a mesh: lat: 8 (over z, core), freq: 4 (over y, x).
Axes of the slice: x: 2, y: 2, z: 4, core: 2. Of those that a mesh axis runs over, the one named last changes fastest.
Arguments:
- wavefield: float32 [2, 8, 2048, 2048], P(None, 'freq', 'lat'), may hold values from -6 to 6
- source_field: float32 [2, 8, 2048, 2048], P(None, 'freq', 'lat'), may hold values from -6 to 6
- slowness: float32 [2048, 2048], P('lat', 'freq'), may hold values from 0.00015 to 0.00094
- freq_index: int32 [8], P('freq'), may hold values from 192 to 767, as said below
Outputs:
- next_field: float32 [2, 8, 2048, 2048], P(None, 'freq', 'lat')
- image: float32 [2048, 2048], P('lat', 'freq')
Inputs may be any that keep to these rules, and one draw needn't show every extreme that they name: `freq_index`: distinct frequency indices.
All inputs are finite; a program needn't handle non-finite values.
Results may differ from a plain program's by a relative error of at most 0.00013.
Values sent between devices are 32-bit elements; how exact they have to be, the bound alone decides.
A program may use at most 128 MiB of HBM per device.

v0:
```python
import functools
import math

import jax
import jax.numpy as jnp
import numpy as np
from jax import lax
from jax.experimental import pallas as pl
from jax.experimental.pallas import tpu as pltpu
from jax.sharding import PartitionSpec as P

depth_step = 10.0
grid_step = 25.0
freq_step = 0.0625
LANES = 128
HALO = 8
VMEM_BYTES = 48 * 1024 * 1024


def dft_tables(sign):
    i = np.arange(LANES)
    ang = 2.0 * math.pi / LANES * ((i[:, None] * i[None, :]) % LANES)
    c, s = np.cos(ang), sign * np.sin(ang)
    return np.block([[c, s], [-s, c]])


def split_table(table):
    high = jnp.asarray(table.astype(np.float32)).astype(jnp.bfloat16)
    high64 = np.asarray(table.astype(np.float32).astype(jnp.bfloat16)).astype(np.float64)
    low = (table - high64).astype(np.float32).astype(jnp.bfloat16)
    return jnp.stack([high, jnp.asarray(low)])


def twiddle(count):
    factor = count // LANES
    k, n = np.arange(factor), np.arange(LANES)
    ang = 2.0 * math.pi / count * ((k[:, None] * n[None, :]) % count)
    return np.stack([np.cos(ang), np.sin(ang)]).astype(np.float32)


def fft_list(values, sign):
    count = len(values)
    if count == 1:
        return values
    even, odd = fft_list(values[0::2], sign), fft_list(values[1::2], sign)
    low, high = [], []
    for k in range(count // 2):
        (er, ei), (r, i) = even[k], odd[k]
        if k == 0:
            tr, ti = r, i
        elif 4 * k == count:
            tr, ti = (-i, r) if sign > 0 else (i, -r)
        else:
            c = math.cos(2.0 * math.pi * k / count)
            s = sign * math.sin(2.0 * math.pi * k / count)
            if abs(abs(c) - abs(s)) < 1e-9:
                h = math.sqrt(0.5)
                sc, ss = (1 if c > 0 else -1), (1 if s > 0 else -1)
                tr = h * (r - i) if sc * ss > 0 else h * (r + i)
                ti = h * (i + r) if sc * ss > 0 else h * (i - r)
                if sc < 0:
                    tr, ti = -tr, -ti
            else:
                tr, ti = c * r - s * i, c * i + s * r
        low.append((er + tr, ei + ti))
        high.append((er - tr, ei - ti))
    return low + high


def sin_cos(angle):
    turns = jnp.round(angle * (0.5 / math.pi))
    r = angle - turns * 6.28125 - turns * (2.0 * math.pi - 6.28125)
    r2 = r * r
    s = jnp.full_like(r, 1.0 / math.factorial(17))
    for n in range(15, 0, -2):
        s = s * r2 + ((-1) ** (n // 2)) / math.factorial(n)
    c = jnp.full_like(r, -1.0 / math.factorial(18))
    for n in range(16, -1, -2):
        c = c * r2 + ((-1) ** (n // 2)) / math.factorial(n)
    return s * r, c


def split(x):
    high = x.astype(jnp.bfloat16)
    return high, (x - high.astype(jnp.float32)).astype(jnp.bfloat16)


def dot(a, b):
    return jnp.dot(a, b, preferred_element_type=jnp.float32)


def forward_kernel(ang_ref, wave_ref, slow_ref, tw_ref, m_ref, out_ref, zs, total, *, member):
    factor, block = zs.shape[0], zs.shape[1]
    part_width, width = slow_ref.shape[2], out_ref.shape[3]
    scale = ang_ref[member] * depth_step
    step = pl.program_id(0)
    start = pl.multiple_of(step * block, block)
    last = pl.num_programs(0) - 1

    @pl.when(step == 0)
    def _():
        total[...] = jnp.zeros_like(total)

    def tile(t, sums):
        rows = pl.ds(pl.multiple_of(t * 8, 8), 8)
        cells = []
        for n in range(factor):
            at = n * LANES
            s = slow_ref[at // part_width, rows, pl.ds(at % part_width, LANES)]
            sums = sums + s
            sn, cs = sin_cos(s * scale)
            re = wave_ref[0, 0, rows, pl.ds(at, LANES)]
            im = wave_ref[1, 0, rows, pl.ds(at, LANES)]
            cells.append((re * cs - im * sn, re * sn + im * cs))
        for k, (re, im) in enumerate(fft_list(cells, -1.0)):
            if k:
                c, s = tw_ref[0, pl.ds(k, 1), :], tw_ref[1, pl.ds(k, 1), :]
                re, im = re * c + im * s, im * c - re * s
            zs[k, rows, pl.ds(0, LANES)] = re
            zs[k, rows, pl.ds(LANES, LANES)] = im
        return sums

    total[...] = lax.fori_loop(0, block // 8, tile, total[...])
    for g in range(0, factor, 4):
        high, low = split(zs[pl.ds(g, 4)].reshape(4 * block, 2 * LANES))
        y = dot(high, m_ref[0]) + (dot(low, m_ref[0]) + dot(high, m_ref[1]))
        y = y.reshape(4, block, 2 * LANES)
        for j in range(4):
            at = (g + j) * LANES
            cols = pl.ds(at % width, LANES)
            out_ref[at // width, 0, pl.ds(start, block), cols] = y[j, :, :LANES]
            out_ref[at // width, 1, pl.ds(start, block), cols] = y[j, :, LANES:]

    if member == 0:
        @pl.when(step == last)
        def _():
            value = jnp.full((HALO, width), jnp.sum(total[...]), jnp.float32)
            for d in range(out_ref.shape[0]):
                for c in range(2):
                    out_ref[d, c, pl.ds(out_ref.shape[2] - HALO, HALO), :] = value


def shift_kernel(ang_ref, mean_ref, in_ref, tw_ref, m_ref, out_ref, zs, *, member):
    factor, width = zs.shape[0], zs.shape[2]
    strips, rows_in = in_ref.shape[0], out_ref.shape[2] - HALO
    count = factor * LANES
    base = lax.axis_index("lat") * width

    def tile_in(t, carry):
        r = pl.multiple_of(t * 8, 8)
        for lane in range(0, width, LANES):
            lanes = pl.ds(lane, LANES)
            cells = []
            for n in range(factor):
                at = n * LANES
                rows = pl.ds(at % rows_in + r, 8)
                cells.append(
                    (in_ref[at // rows_in, 0, rows, lanes], in_ref[at // rows_in, 1, rows, lanes])
                )
            for k, (re, im) in enumerate(fft_list(cells, -1.0)):
                if k:
                    c, s = tw_ref[0, k, pl.ds(r, 8), :], tw_ref[1, k, pl.ds(r, 8), :]
                    re, im = re * c + im * s, im * c - re * s
                zs[k, pl.ds(r, 8), lanes] = re
                zs[k, pl.ds(LANES + r, 8), lanes] = im
        return carry

    lax.fori_loop(0, LANES // 8, tile_in, 0)

    angular_mean = ang_ref[member] * mean_ref[0]
    flat = angular_mean * depth_step
    place = base + lax.broadcasted_iota(jnp.int32, (LANES, width), 1)
    index_y = place // LANES + factor * (place % LANES)
    signed_y = jnp.where(index_y < count // 2, index_y, index_y - count)
    wave_y = 2.0 * math.pi / (count * grid_step) * signed_y.astype(jnp.float32)
    rest = angular_mean * angular_mean - wave_y * wave_y
    row = lax.broadcasted_iota(jnp.int32, (LANES, width), 0)

    def product(k, carry):
        high, low = split(zs[k])
        y = dot(m_ref[0], high) + (dot(m_ref[0], low) + dot(m_ref[1], high))
        index_x = k + factor * row
        signed_x = jnp.where(index_x < count // 2, index_x, index_x - count)
        wave_x = 2.0 * math.pi / (count * grid_step) * signed_x.astype(jnp.float32)
        vertical = rest - wave_x * wave_x
        size = jnp.sqrt(jnp.abs(vertical)) * depth_step
        damping = jnp.where(vertical < 0.0, jnp.exp(-size), 1.0) * (1.0 / (count * count))
        sn, cs = sin_cos(jnp.where(vertical > 0.0, size, 0.0) - flat)
        tr, ti = damping * cs, damping * sn
        re, im = y[:LANES], y[LANES:]
        z = jnp.concatenate([re * tr - im * ti, re * ti + im * tr], axis=0)
        high, low = split(z)
        zs[k] = dot(m_ref[2], high) + (dot(m_ref[2], low) + dot(m_ref[3], high))
        return carry

    lax.fori_loop(0, factor, product, 0)

    def tile_out(t, carry):
        r = pl.multiple_of(t * 8, 8)
        for lane in range(0, width, LANES):
            lanes = pl.ds(lane, LANES)
            cells = []
            for k in range(factor):
                re, im = zs[k, pl.ds(r, 8), lanes], zs[k, pl.ds(LANES + r, 8), lanes]
                if k:
                    c, s = tw_ref[0, k, pl.ds(r, 8), :], tw_ref[1, k, pl.ds(r, 8), :]
                    re, im = re * c - im * s, im * c + re * s
                cells.append((re, im))
            for n, (re, im) in enumerate(fft_list(cells, 1.0)):
                at = n * LANES
                rows = pl.ds(at % rows_in + r, 8)
                out_ref[at // rows_in, 0, rows, lanes] = re
                out_ref[at // rows_in, 1, rows, lanes] = im
        return carry

    lax.fori_loop(0, LANES // 8, tile_out, 0)
    for d in range(strips):
        for c in range(2):
            out_ref[d, c, pl.ds(rows_in, HALO), :] = jnp.zeros((HALO, width), jnp.float32)
            if d > 0:
                out_ref[d, c, pl.ds(rows_in, 1), :] = out_ref[d - 1, c, pl.ds(rows_in - 1, 1), :]
            if d < strips - 1:
                out_ref[d, c, pl.ds(rows_in + 1, 1), :] = out_ref[d + 1, c, pl.ds(0, 1), :]


def finish_kernel(
    ang_ref, mean_ref, in_ref, src_ref, slow_ref, tw_ref, m_ref, *rest, member, batch_total
):
    if member:
        _, before_ref, out_ref, term_ref, zs, field = rest
    else:
        out_ref, term_ref, zs, field = rest
    factor, tall = zs.shape[0], zs.shape[1]
    rows_in, width = tall - HALO, in_ref.shape[3]
    block, part_width = term_ref.shape[1:]
    full = field.shape[2]
    step = pl.program_id(0)

    @pl.when(step == 0)
    def _():
        for k in range(factor):
            at = k * LANES
            cols = pl.ds(at % width, LANES)
            x = jnp.concatenate(
                [in_ref[at // width, 0, :, cols], in_ref[at // width, 1, :, cols]], axis=1
            )
            high, low = split(x)
            zs[k] = dot(high, m_ref[0]) + (dot(low, m_ref[0]) + dot(high, m_ref[1]))

        def columns(rows):
            cells = []
            for k in range(factor):
                re, im = zs[k, rows, pl.ds(0, LANES)], zs[k, rows, pl.ds(LANES, LANES)]
                if k:
                    c, s = tw_ref[0, pl.ds(k, 1), :], tw_ref[1, pl.ds(k, 1), :]
                    re, im = re * c - im * s, im * c + re * s
                cells.append((re, im))
            return fft_list(cells, 1.0)

        def tile(t, carry):
            r = pl.multiple_of(t * 8, 8)
            for n, pair in enumerate(columns(pl.ds(r, 8))):
                for c in range(2):
                    field[c, pl.ds(8 + r, 8), pl.ds(n * LANES, LANES)] = pair[c]
            return carry

        lax.fori_loop(0, rows_in // 8, tile, 0)
        for n, pair in enumerate(columns(pl.ds(rows_in, 8))):
            for c in range(2):
                field[c, pl.ds(7, 1), pl.ds(n * LANES, LANES)] = pair[c][0:1]
                field[c, pl.ds(8 + rows_in, 1), pl.ds(n * LANES, LANES)] = pair[c][1:2]

    angular = ang_ref[member]
    ahead = 0.5 / (angular * mean_ref[0])
    column = lax.broadcasted_iota(jnp.int32, (block, full), 1)
    start = pl.multiple_of(step * block, 8)
    centre, laplace = [], []
    for c in range(2):
        cells = field[c, pl.ds(start, block + 16), :]
        mid = cells[8 : 8 + block]
        up = pltpu.roll(cells, 1, 0)[8 : 8 + block]
        down = pltpu.roll(cells, block + 15, 0)[8 : 8 + block]
        left = jnp.where(column == 0, 0.0, pltpu.roll(mid, 1, 1))
        right = jnp.where(column == full - 1, 0.0, pltpu.roll(mid, full - 1, 1))
        centre.append(mid)
        laplace.append(up + down + left + right - 4.0 * mid)
    slow = jnp.concatenate([slow_ref[p] for p in range(slow_ref.shape[0])], axis=1)
    gain = (ahead - 0.5 / (angular * slow)) * (depth_step / (grid_step * grid_step))
    new_re = centre[0] + gain * laplace[1]
    new_im = centre[1] - gain * laplace[0]
    out_ref[0, 0] = new_re
    out_ref[1, 0] = new_im
    term = (new_re * src_ref[0, 0] + new_im * src_ref[1, 0]) * (1.0 / math.sqrt(batch_total))
    for p in range(slow_ref.shape[0]):
        part = term[:, p * part_width : (p + 1) * part_width]
        term_ref[p] = part + before_ref[p] if member else part


def params():
    return pltpu.CompilerParams(vmem_limit_bytes=VMEM_BYTES)


def whole(array):
    zeros = (0,) * array.ndim
    return pl.BlockSpec(array.shape, lambda *_: zeros)


SMEM = pl.BlockSpec(memory_space=pltpu.SMEM)


def local(wavefield, source_field, slowness, freq_index):
    _, members, rows, full = wavefield.shape
    strips, groups = lax.axis_size("lat"), lax.axis_size("freq")
    width = full // strips
    factor = full // LANES
    part_width = full // groups
    count_x = rows * strips
    angular = 2.0 * math.pi * freq_step * freq_index.astype(jnp.float32)
    tw = twiddle(full)
    tw_row = jnp.asarray(tw)
    tw_x = jnp.asarray(np.ascontiguousarray(np.broadcast_to(tw[..., None], tw.shape + (LANES,))))
    right_fwd, right_inv = dft_tables(-1.0), dft_tables(1.0)
    m_fwd, m_inv = split_table(right_fwd), split_table(right_inv)
    m_both = jnp.concatenate(
        [split_table(np.ascontiguousarray(right_fwd.T)), split_table(np.ascontiguousarray(right_inv.T))]
    )
    copies = jnp.broadcast_to(slowness, (groups,) + slowness.shape)
    strip = lax.all_to_all(copies, "freq", split_axis=0, concat_axis=0, tiled=True)

    block = 128

    def forward(member):
        tall = rows + HALO if member == 0 else rows
        return pl.pallas_call(
            functools.partial(forward_kernel, member=member),
            grid=(rows // block,),
            in_specs=[
                SMEM,
                pl.BlockSpec((2, 1, block, full), lambda i: (0, member, i, 0)),
                pl.BlockSpec((groups, block, part_width), lambda i: (0, i, 0)),
                whole(tw_row),
                whole(m_fwd),
            ],
            out_specs=pl.BlockSpec((strips, 2, tall, width), lambda i: (0, 0, 0, 0)),
            out_shape=jax.ShapeDtypeStruct((strips, 2, tall, width), jnp.float32),
            scratch_shapes=[
                pltpu.VMEM((factor, block, 2 * LANES), jnp.float32),
                pltpu.VMEM((8, LANES), jnp.float32),
            ],
            compiler_params=params(),
            cost_estimate=pl.CostEstimate(
                flops=4_000_000_000, bytes_accessed=40_000_000, transcendentals=0
            ),
            name="forward",
        )(angular, wavefield, strip, tw_row, m_fwd)

    def shift(member, mean_slow, spectra):
        return pl.pallas_call(
            functools.partial(shift_kernel, member=member),
            grid=(1,),
            in_specs=[SMEM, SMEM, whole(spectra), whole(tw_x), whole(m_both)],
            out_specs=pl.BlockSpec((strips, 2, rows + HALO, width), lambda i: (0, 0, 0, 0)),
            out_shape=jax.ShapeDtypeStruct((strips, 2, rows + HALO, width), jnp.float32),
            scratch_shapes=[pltpu.VMEM((factor, 2 * LANES, width), jnp.float32)],
            compiler_params=params(),
            cost_estimate=pl.CostEstimate(
                flops=10_000_000_000, bytes_accessed=100_000_000, transcendentals=0
            ),
            name="shift",
        )(angular, mean_slow, spectra, tw_x, m_both)

    final_block = 64

    def finish(member, mean_slow, lines, before):
        strip_block = pl.BlockSpec((groups, final_block, part_width), lambda i: (0, i, 0))
        field_block = pl.BlockSpec((2, 1, final_block, full), lambda i: (0, member, i, 0))
        specs = [SMEM, SMEM, whole(lines), field_block, strip_block, whole(tw_row), whole(m_inv)]
        arrays = [angular, mean_slow, lines, source_field, strip, tw_row, m_inv]
        aliases = {}
        if member:
            aliases = {len(arrays): 0}
            specs += [pl.BlockSpec(memory_space=pl.ANY), strip_block]
            arrays += list(before)
        return pl.pallas_call(
            functools.partial(
                finish_kernel, member=member, batch_total=members * groups
            ),
            grid=(rows // final_block,),
            in_specs=specs,
            out_specs=[field_block, strip_block],
            out_shape=[
                jax.ShapeDtypeStruct((2, members, rows, full), jnp.float32),
                jax.ShapeDtypeStruct((groups, rows, part_width), jnp.float32),
            ],
            scratch_shapes=[
                pltpu.VMEM((factor, rows + HALO, 2 * LANES), jnp.float32),
                pltpu.VMEM((2, rows + 16, full), jnp.float32),
            ],
            input_output_aliases=aliases,
            compiler_params=params(),
            cost_estimate=pl.CostEstimate(
                flops=8_000_000_000, bytes_accessed=80_000_000, transcendentals=0
            ),
            name="finish",
        )(*arrays)

    def exchange(cells):
        return lax.all_to_all(cells, "lat", split_axis=0, concat_axis=0, tiled=True)

    spectra = [forward(m) for m in range(members)]
    lines = [exchange(s) for s in spectra]
    total = jnp.sum(lax.slice(lines[0], (0, 0, rows, 0), (strips, 1, rows + 1, 1)))
    mean_slow = (total / (count_x * full)).reshape(1)
    shifted = [exchange(shift(m, mean_slow, lines[m])) for m in range(members)]
    state = None
    for m in range(members):
        state = finish(m, mean_slow, shifted[m], state)
    field, terms = state
    image = jnp.sum(
        lax.all_to_all(terms, "freq", split_axis=0, concat_axis=0, tiled=True), axis=0
    )
    return (field, image)


def solution(mesh):
    return jax.shard_map(
        local,
        mesh=mesh,
        in_specs=(
            P(None, "freq", "lat", None),
            P(None, "freq", "lat", None),
            P("lat", "freq"),
            P("freq"),
        ),
        out_specs=(P(None, "freq", "lat", None), P("lat", "freq")),
        check_vma=False,
    )
```

profile of v0, /device:TPU:0, one launch (start us, length us, event | category | flops | bytes accessed | tf_op | source)
XLA Modules:
  0.0 488.3 jit_solution(702544276225357966)
XLA Ops:
  0.6 0.0 copy-start.1
  0.6 0.0 copy-start
  0.7 0.0 copy-start.7
  0.7 2.7 broadcast_in_dim.3
  3.3 5.2 %all-to-all-start = ((f32[4,256,512]{2,1,0:T(8,128)}), f32[4,256,512]{2,1,0:T(8,128)S(1)}, u32[]{:S(2)}, u32[]{:S(2)}) async-start(f32[4,256,512]{2,1,0:T(8,128)} %broadcast_in_dim.3), calls=%async_computation | async-start | bytes 4194304 | tf_op jit(solution)/shard_map/all_to_all | solution.py:328
  8.5 0.0 copy-done.7
  8.5 24.9 %all-to-all-done.slow_ref = f32[4,256,512]{2,1,0:T(8,128)S(1)} async-done(((f32[4,256,512]{2,1,0:T(8,128)}), f32[4,256,512]{2,1,0:T(8,128)S(1)}, u32[]{:S(2)}, u32[]{:S(2)}) %all-to-all-start) | async-done | bytes 2097184 | tf_op jit(solution)/shard_map/all_to_all | solution.py:328
  33.4 0.0 copy-done.1
  33.4 0.0 copy-done
  33.4 10.6 %forward.2 = f32[8,2,264,256]{3,2,1,0:T(8,128)} custom-call(f32[2]{0:T(128)S(1)} %convert_multiply_fusion.ang_ref, f32[2,2,256,2048]{3,2,1,0:T(8,128)} %wave_ref.3, f32[4,256,512]{2,1,0:T(8,128)S(1)} %all-to-all-done.slow_ref, f32[2,16,128]{2,1,0:T(8,128)S(1)} %copy-done.1, bf16[2,256,256]{2,1,0:T(8,128)(2,1)S(1)} %copy-done), custom_call_target="tpu_custom_call" | custom-call | flops 4000000000 | bytes 40000000 | tf_op jit(solution)/shard_map/forward/pallas_call | solution.py:334
  44.0 5.0 %all-to-all-start.1 = ((f32[8,2,264,256]{3,2,1,0:T(8,128)}), f32[8,2,264,256]{3,2,1,0:T(8,128)}, u32[]{:S(2)}, u32[]{:S(2)}) async-start(f32[8,2,264,256]{3,2,1,0:T(8,128)} %forward.2), calls=%async_computation.1 | async-start | bytes 8650752 | tf_op jit(solution)/shard_map/all_to_all | solution.py:408
  49.0 10.5 %forward.3 = f32[8,2,256,256]{3,2,1,0:T(8,128)} custom-call(f32[2]{0:T(128)S(1)} %convert_multiply_fusion.ang_ref, f32[2,2,256,2048]{3,2,1,0:T(8,128)} %wave_ref.3, f32[4,256,512]{2,1,0:T(8,128)S(1)} %all-to-all-done.slow_ref, f32[2,16,128]{2,1,0:T(8,128)S(1)} %copy-done.1, bf16[2,256,256]{2,1,0:T(8,128)(2,1)S(1)} %copy-done), custom_call_target="tpu_custom_call" | custom-call | flops 4000000000 | bytes 40000000 | tf_op jit(solution)/shard_map/forward/pallas_call | solution.py:334
  59.5 0.0 copy-start.4
  59.5 86.5 %all-to-all-done.1.in_ref = f32[8,2,264,256]{3,2,1,0:T(8,128)} async-done(((f32[8,2,264,256]{3,2,1,0:T(8,128)}), f32[8,2,264,256]{3,2,1,0:T(8,128)}, u32[]{:S(2)}, u32[]{:S(2)}) %all-to-all-start.1) | async-done | bytes 4325408 | tf_op jit(solution)/shard_map/all_to_all | solution.py:408
  146.0 4.6 all-to-all-start.2
  150.5 1.4 slice_reduce_fusion
  152.6 0.0 copy-done.4
  152.6 0.0 copy-start.2
  152.6 1.6 copy-done.2
  154.2 21.2 %shift.3 = f32[8,2,264,256]{3,2,1,0:T(8,128)} custom-call(f32[2]{0:T(128)S(1)} %convert_multiply_fusion.ang_ref, f32[1]{0:T(128)} %bitcast.mean_ref, f32[8,2,264,256]{3,2,1,0:T(8,128)} %all-to-all-done.1.in_ref, f32[2,16,128,128]{3,2,1,0:T(8,128)S(1)} %copy-done.2, bf16[4,256,256]{2,1,0:T(8,128)(2,1)S(1)} %copy-done.4), custom_call_target="tpu_custom_call" | custom-call | flops 10000000000 | bytes 100000000 | tf_op jit(solution)/shard_map/shift/pallas_call | solution.py:358
  175.3 69.2 %all-to-all-done.2.in_ref = f32[8,2,256,256]{3,2,1,0:T(8,128)} async-done(((f32[8,2,256,256]{3,2,1,0:T(8,128)}), f32[8,2,256,256]{3,2,1,0:T(8,128)}, u32[]{:S(2)}, u32[]{:S(2)}) %all-to-all-start.2) | async-done | bytes 4194336 | tf_op jit(solution)/shard_map/all_to_all | solution.py:408
  244.5 4.6 all-to-all-start.4
  249.2 0.0 copy-start.3
  249.2 1.6 copy-done.3
  250.8 21.1 %shift.2 = f32[8,2,264,256]{3,2,1,0:T(8,128)} custom-call(f32[2]{0:T(128)S(1)} %convert_multiply_fusion.ang_ref, f32[1]{0:T(128)} %bitcast.mean_ref, f32[8,2,256,256]{3,2,1,0:T(8,128)} %all-to-all-done.2.in_ref, f32[2,16,128,128]{3,2,1,0:T(8,128)S(1)} %copy-done.3, bf16[4,256,256]{2,1,0:T(8,128)(2,1)S(1)} %copy-done.4), custom_call_target="tpu_custom_call" | custom-call | flops 10000000000 | bytes 100000000 | tf_op jit(solution)/shard_map/shift/pallas_call | solution.py:358
  271.9 0.0 copy-start.5
  271.9 74.1 %all-to-all-done.4.in_ref = f32[8,2,264,256]{3,2,1,0:T(8,128)} async-done(((f32[8,2,264,256]{3,2,1,0:T(8,128)}), f32[8,2,264,256]{3,2,1,0:T(8,128)}, u32[]{:S(2)}, u32[]{:S(2)}) %all-to-all-start.4) | async-done | bytes 4325408 | tf_op jit(solution)/shard_map/all_to_all | solution.py:408
  346.0 4.6 all-to-all-start.3
  350.6 0.0 copy-done.5
  350.6 11.6 %finish.2 = (f32[2,2,256,2048]{3,2,1,0:T(8,128)}, f32[4,256,512]{2,1,0:T(8,128)S(1)}) custom-call(f32[2]{0:T(128)S(1)} %convert_multiply_fusion.ang_ref, f32[1]{0:T(128)} %bitcast.mean_ref, f32[8,2,264,256]{3,2,1,0:T(8,128)} %all-to-all-done.4.in_ref, f32[2,2,256,2048]{3,2,1,0:T(8,128)} %src_ref.3, f32[4,256,512]{2,1,0:T(8,128)S(1)} %all-to-all-done.slow_ref, ...), custom_call_target="tpu_custom_call" | custom-call | flops 8000000000 | bytes 80000000 | tf_op jit(solution)/shard_map/finish/pallas_call | solution.py:384
  362.1 0.0 copy-start.6
  362.1 1.4 copy-done.6
  363.5 83.9 %all-to-all-done.3.in_ref = f32[8,2,264,256]{3,2,1,0:T(8,128)} async-done(((f32[8,2,264,256]{3,2,1,0:T(8,128)}), f32[8,2,264,256]{3,2,1,0:T(8,128)}, u32[]{:S(2)}, u32[]{:S(2)}) %all-to-all-start.3) | async-done | bytes 4325408 | tf_op jit(solution)/shard_map/all_to_all | solution.py:408
  447.4 12.0 %finish.3 = (f32[2,2,256,2048]{3,2,1,0:T(8,128)}, f32[4,256,512]{2,1,0:T(8,128)S(1)}) custom-call(f32[2]{0:T(128)S(1)} %convert_multiply_fusion.ang_ref, f32[1]{0:T(128)} %bitcast.mean_ref, f32[8,2,264,256]{3,2,1,0:T(8,128)} %all-to-all-done.3.in_ref, f32[2,2,256,2048]{3,2,1,0:T(8,128)} %src_ref.3, ...), custom_call_target="tpu_custom_call", output_to_operand_aliasing={{0}: (7, {})} | custom-call | flops 8000000000 | bytes 80000000 | tf_op jit(solution)/shard_map/finish/pallas_call | solution.py:384
  459.4 27.9 %all_to_all.30 = f32[4,256,512]{2,1,0:T(8,128)S(1)} all-to-all(f32[4,256,512]{2,1,0:T(8,128)S(1)} %get-tuple-element.9), channel_id=1, replica_groups=mesh['lat'=8,'freq'=4] {'freq'}, dimensions={0} | all-to-all | bytes 4194304 | tf_op jit(solution)/shard_map/all_to_all | solution.py:420
  487.3 1.0 reduce_sum.19
  (1 shorter events, 0.0 us)
Async XLA Ops:
  0.6 32.7 %copy-start.1 = (f32[2,16,128]{2,1,0:T(8,128)S(1)}, f32[2,16,128]{2,1,0:T(8,128)}, u32[]{:S(2)}) copy-start(f32[2,16,128]{2,1,0:T(8,128)} %constant.19.clone.tw_ref) | copy-start | bytes 49156
  0.6 32.7 %copy-start = (bf16[2,256,256]{2,1,0:T(8,128)(2,1)S(1)}, bf16[2,256,256]{2,1,0:T(8,128)(2,1)}, u32[]{:S(2)}) copy-start(bf16[2,256,256]{2,1,0:T(8,128)(2,1)} %constant.31.m_ref) | copy-start | bytes 786436
  0.7 7.9 %copy-start.7 = (s32[2]{0:T(128)S(1)}, s32[2]{0:T(128)}, u32[]{:S(2)}) copy-start(s32[2]{0:T(128)} %param.17) | copy-start | bytes 28
  3.3 30.0 %all-to-all-start = ((f32[4,256,512]{2,1,0:T(8,128)}), f32[4,256,512]{2,1,0:T(8,128)S(1)}, u32[]{:S(2)}, u32[]{:S(2)}) async-start(f32[4,256,512]{2,1,0:T(8,128)} %broadcast_in_dim.3), calls=%async_computation | async-start | bytes 4194304 | tf_op jit(solution)/shard_map/all_to_all | solution.py:328
  44.0 101.9 %all-to-all-start.1 = ((f32[8,2,264,256]{3,2,1,0:T(8,128)}), f32[8,2,264,256]{3,2,1,0:T(8,128)}, u32[]{:S(2)}, u32[]{:S(2)}) async-start(f32[8,2,264,256]{3,2,1,0:T(8,128)} %forward.2), calls=%async_computation.1 | async-start | bytes 8650752 | tf_op jit(solution)/shard_map/all_to_all | solution.py:408
  59.5 93.1 %copy-start.4 = (bf16[4,256,256]{2,1,0:T(8,128)(2,1)S(1)}, bf16[4,256,256]{2,1,0:T(8,128)(2,1)}, u32[]{:S(2)}) copy-start(bf16[4,256,256]{2,1,0:T(8,128)(2,1)} %constant.35.m_ref) | copy-start | bytes 1572868
  146.0 98.6 %all-to-all-start.2 = ((f32[8,2,256,256]{3,2,1,0:T(8,128)}), f32[8,2,256,256]{3,2,1,0:T(8,128)}, u32[]{:S(2)}, u32[]{:S(2)}) async-start(f32[8,2,256,256]{3,2,1,0:T(8,128)} %forward.3), calls=%async_computation.2 | async-start | bytes 8388608 | tf_op jit(solution)/shard_map/all_to_all | solution.py:408
  152.6 1.6 copy-start.2
  244.5 101.5 %all-to-all-start.4 = ((f32[8,2,264,256]{3,2,1,0:T(8,128)}), f32[8,2,264,256]{3,2,1,0:T(8,128)}, u32[]{:S(2)}, u32[]{:S(2)}) async-start(f32[8,2,264,256]{3,2,1,0:T(8,128)} %shift.3), calls=%async_computation.4 | async-start | bytes 8650752 | tf_op jit(solution)/shard_map/all_to_all | solution.py:408
  249.2 1.6 copy-start.3
  271.9 78.7 %copy-start.5 = (bf16[2,256,256]{2,1,0:T(8,128)(2,1)S(1)}, bf16[2,256,256]{2,1,0:T(8,128)(2,1)}, u32[]{:S(2)}) copy-start(bf16[2,256,256]{2,1,0:T(8,128)(2,1)} %constant.36.m_ref) | copy-start | bytes 786436
  346.0 101.4 %all-to-all-start.3 = ((f32[8,2,264,256]{3,2,1,0:T(8,128)}), f32[8,2,264,256]{3,2,1,0:T(8,128)}, u32[]{:S(2)}, u32[]{:S(2)}) async-start(f32[8,2,264,256]{3,2,1,0:T(8,128)} %shift.2), calls=%async_computation.3 | async-start | bytes 8650752 | tf_op jit(solution)/shard_map/all_to_all | solution.py:408
  362.1 1.4 copy-start.6
where the time goes:
time: 489 us; the launch traced here: 488 us
  waiting for transfers between devices  338 us (69%)
  Pallas kernels  86.9 us (18%)
  blocking collectives  27.9 us (6%)
  starting transfers between devices  24 us (5%)
  local copies, waits for them, and re-layouts  7.25 us (1%)
    all_to_all x4, waiting for transfers between devices, exchange(): return lax.all_to_all(cells, 'lat', split_axis=0, concat_axis=0, tiled=True)  314 us
    pallas_call x2, Pallas kernels, shift(): pl.pallas_call(functools.partial(shift_kernel, member=member), grid=(1,),...  42.3 us
    all_to_all x1, blocking collectives, local(): lax.all_to_all(terms, 'freq', split_axis=0, concat_axis=0, tiled=True)  27.9 us
    all_to_all x1, waiting for transfers between devices, local(): lax.all_to_all(copies, 'freq', split_axis=0, concat_axis=0, tiled=True)  24.9 us
    pallas_call x2, Pallas kernels, finish(): pl.pallas_call(functools.partial(finish_kernel, member=member, batch_tota...  23.6 us
    pallas_call x2, Pallas kernels, forward(): pl.pallas_call(functools.partial(forward_kernel, member=member), grid=(ro...  21.1 us
    all_to_all x4, starting transfers between devices, exchange(): return lax.all_to_all(cells, 'lat', split_axis=0, concat_axis=0, tiled=True)  18.8 us
  transfers between devices with their start and end apart: 5, of which 5 were waited for; matrix products, arithmetic and copies ran while one was open for 0% of the time, Pallas kernels for 13%

commit v1 on v0

v1 whole, which is shorter than its diff:
```python
import functools
import math

import jax
import jax.numpy as jnp
import numpy as np
from jax import lax
from jax.experimental import pallas as pl
from jax.experimental.pallas import tpu as pltpu
from jax.sharding import PartitionSpec as P

depth_step = 10.0
grid_step = 25.0
freq_step = 0.0625
LANES = 128
CHUNK = 32
VMEM_BYTES = 60 * 1024 * 1024
MESH = pl.DeviceIdType.MESH


def dft_tables(sign):
    i = np.arange(LANES)
    ang = 2.0 * math.pi / LANES * ((i[:, None] * i[None, :]) % LANES)
    c, s = np.cos(ang), sign * np.sin(ang)
    return np.block([[c, s], [-s, c]])


def split_table(table):
    high = jnp.asarray(table.astype(np.float32)).astype(jnp.bfloat16)
    high64 = np.asarray(table.astype(np.float32).astype(jnp.bfloat16)).astype(np.float64)
    low = (table - high64).astype(np.float32).astype(jnp.bfloat16)
    return jnp.stack([high, jnp.asarray(low)])


def twiddle(count):
    factor = count // LANES
    k, n = np.arange(factor), np.arange(LANES)
    ang = 2.0 * math.pi / count * ((k[:, None] * n[None, :]) % count)
    return np.stack([np.cos(ang), np.sin(ang)]).astype(np.float32)


def fft_list(values, sign):
    count = len(values)
    if count == 1:
        return values
    even, odd = fft_list(values[0::2], sign), fft_list(values[1::2], sign)
    low, high = [], []
    for k in range(count // 2):
        (er, ei), (r, i) = even[k], odd[k]
        if k == 0:
            tr, ti = r, i
        elif 4 * k == count:
            tr, ti = (-i, r) if sign > 0 else (i, -r)
        else:
            c = math.cos(2.0 * math.pi * k / count)
            s = sign * math.sin(2.0 * math.pi * k / count)
            if abs(abs(c) - abs(s)) < 1e-9:
                h = math.sqrt(0.5)
                sc, ss = (1 if c > 0 else -1), (1 if s > 0 else -1)
                tr = h * (r - i) if sc * ss > 0 else h * (r + i)
                ti = h * (i + r) if sc * ss > 0 else h * (i - r)
                if sc < 0:
                    tr, ti = -tr, -ti
            else:
                tr, ti = c * r - s * i, c * i + s * r
        low.append((er + tr, ei + ti))
        high.append((er - tr, ei - ti))
    return low + high


def sin_cos(angle):
    turns = jnp.round(angle * (0.5 / math.pi))
    r = angle - turns * 6.28125 - turns * (2.0 * math.pi - 6.28125)
    r2 = r * r
    s = jnp.full_like(r, 1.0 / math.factorial(17))
    for n in range(15, 0, -2):
        s = s * r2 + ((-1) ** (n // 2)) / math.factorial(n)
    c = jnp.full_like(r, -1.0 / math.factorial(18))
    for n in range(16, -1, -2):
        c = c * r2 + ((-1) ** (n // 2)) / math.factorial(n)
    return s * r, c


def split(x):
    high = x.astype(jnp.bfloat16)
    return high, (x - high.astype(jnp.float32)).astype(jnp.bfloat16)


def dot(a, b):
    return jnp.dot(a, b, preferred_element_type=jnp.float32)


def flipped(index, mask, count):
    other, bit = index, 1
    while bit < count:
        if mask & bit:
            other = other + bit * (1 - 2 * ((index // bit) % 2))
        bit *= 2
    return other


def step_kernel(
    freq_ref, wave_hbm, src_hbm, slow_hbm, twx_hbm, tw_ref, m_fwd, m_both, m_inv,
    field_hbm, image_hbm,
    spec_out, spec_in, line_out, line_in, edge_out, edge_in, stat_out, stat_in,
    slow, terms, terms_in, zs, zc, ze, field, twx, wave, source, fresh, picture,
    wave_sem, source_sem, fresh_sem, image_sem, twx_sem, own_sem,
    slow_send, slow_recv, spec_send, spec_recv, spec_own, line_send, line_recv, line_own,
    edge_send, edge_recv, edge_own, stat_send, stat_recv, term_send, term_recv,
    *, batch_total,
):
    members, strips, rows_in, width = (spec_out.shape[i] for i in (0, 1, 3, 4))
    groups, part_width = slow.shape[0], slow.shape[2]
    full = strips * width
    factor = full // LANES
    count = rows_in * strips
    blocks = rows_in // CHUNK
    lane_blocks = width // LANES
    lat, fr = lax.axis_index("lat"), lax.axis_index("freq")
    lat_masks = sorted(range(1, strips), key=lambda m: -m)
    freq_masks = list(range(1, groups))

    def lat_peer(mask):
        return flipped(lat, mask, strips)

    def freq_peer(mask):
        return flipped(fr, mask, groups)

    def chunk_rows(i):
        return pl.ds(pl.multiple_of(i * CHUNK, CHUNK), CHUNK)

    def remote(a, b, send, recv, to):
        return pltpu.make_async_remote_copy(
            src_ref=a, dst_ref=b, send_sem=send, recv_sem=recv, device_id=to, device_id_type=MESH
        )

    def wave_copy(n):
        rows = chunk_rows(n % blocks)
        return pltpu.make_async_copy(
            wave_hbm.at[:, n // blocks, rows, :], wave.at[n % 2], wave_sem.at[n % 2]
        )

    def source_copy(n):
        rows = chunk_rows(n % blocks)
        return pltpu.make_async_copy(
            src_hbm.at[:, n // blocks, rows, :], source.at[n % 2], source_sem.at[n % 2]
        )

    def fresh_copy(n):
        rows = chunk_rows(n % blocks)
        return pltpu.make_async_copy(
            fresh.at[n % 2], field_hbm.at[:, n // blocks, rows, :], fresh_sem.at[n % 2]
        )

    own_slow = pltpu.make_async_copy(slow_hbm, slow.at[fr], own_sem)
    own_slow.start()
    wave_copy(0).start()
    source_copy(0).start()
    twx_copy = pltpu.make_async_copy(twx_hbm, twx, twx_sem)

    barrier = pltpu.get_barrier_semaphore()
    for mask in freq_masks:
        pl.semaphore_signal(barrier, inc=1, device_id=(lat, freq_peer(mask)), device_id_type=MESH)
    for mask in lat_masks:
        pl.semaphore_signal(barrier, inc=1, device_id=(lat_peer(mask), fr), device_id_type=MESH)
    pl.semaphore_wait(barrier, len(freq_masks) + len(lat_masks))

    def send_slow(i, carry):
        rows = chunk_rows(i)
        for mask in freq_masks:
            remote(
                slow_hbm.at[rows, :], slow.at[fr, rows, :], slow_send, slow_recv.at[i],
                (lat, freq_peer(mask)),
            ).start()
        return carry

    lax.fori_loop(0, blocks, send_slow, 0)
    own_slow.wait()

    def forward(n, carry):
        m, i = n // blocks, n % blocks
        rows = chunk_rows(i)

        @pl.when(n + 1 < members * blocks)
        def _():
            wave_copy(n + 1).start()

        @pl.when(n < blocks)
        def _():
            some = slow.at[pl.ds(0, groups - 1), rows, :]
            remote(some, some, slow_send, slow_recv.at[i], (lat, fr)).wait_recv()

        wave_copy(n).wait()
        scale = 2.0 * math.pi * freq_step * freq_ref[m].astype(jnp.float32) * depth_step
        slot = n % 2

        def tile(t, c0):
            r = pl.multiple_of(t * 8, 8)
            at_slow = pl.ds(pl.multiple_of(i * CHUNK + t * 8, 8), 8)
            cells = []
            for k in range(factor):
                at = k * LANES
                s = slow[at // part_width, at_slow, pl.ds(at % part_width, LANES)]
                sn, cs = sin_cos(s * scale)
                re = wave[slot, 0, pl.ds(r, 8), pl.ds(at, LANES)]
                im = wave[slot, 1, pl.ds(r, 8), pl.ds(at, LANES)]
                cells.append((re * cs - im * sn, re * sn + im * cs))
            for k, (re, im) in enumerate(fft_list(cells, -1.0)):
                if k:
                    c, s = tw_ref[0, pl.ds(k, 1), :], tw_ref[1, pl.ds(k, 1), :]
                    re, im = re * c + im * s, im * c - re * s
                zc[k, pl.ds(r, 8), pl.ds(0, LANES)] = re
                zc[k, pl.ds(r, 8), pl.ds(LANES, LANES)] = im
            return c0

        lax.fori_loop(0, CHUNK // 8, tile, 0)
        high, low = split(zc[...].reshape(factor * CHUNK, 2 * LANES))
        y = dot(high, m_fwd[0]) + (dot(low, m_fwd[0]) + dot(high, m_fwd[1]))
        y = y.reshape(factor, CHUNK, 2 * LANES)
        for k in range(factor):
            at = k * LANES
            cols = pl.ds(at % width, LANES)
            spec_out[m, at // width, 0, rows, cols] = y[k, :, :LANES]
            spec_out[m, at // width, 1, rows, cols] = y[k, :, LANES:]
        for mask in lat_masks:
            to = lat_peer(mask)
            remote(
                spec_out.at[m, to, :, rows, :], spec_in.at[m, lat, :, rows, :],
                spec_send.at[m], spec_recv.at[m, lat], (to, fr),
            ).start()
        pltpu.make_async_copy(
            spec_out.at[m, lat, :, rows, :], spec_in.at[m, lat, :, rows, :], spec_own.at[m]
        ).start()

        @pl.when(n == blocks - 1)
        def _():
            def add(t, sums):
                at_slow = pl.ds(pl.multiple_of(t * 8, 8), 8)
                for p in range(groups):
                    for at in range(0, part_width, LANES):
                        sums = sums + slow[p, at_slow, pl.ds(at, LANES)]
                return sums

            total = lax.fori_loop(0, rows_in // 8, add, jnp.zeros((8, LANES), jnp.float32))
            stat_out[...] = total
            stat_in[lat] = total
            for mask in lat_masks:
                remote(
                    stat_out, stat_in.at[lat], stat_send, stat_recv, (lat_peer(mask), fr)
                ).start()

        return carry

    lax.fori_loop(0, members * blocks, forward, 0)

    twx_copy.start()
    some = stat_in.at[pl.ds(0, strips - 1)]
    remote(some, some, stat_send, stat_recv, (lat, fr)).wait_recv()
    twx_copy.wait()
    mean = jnp.sum(stat_in[...]) * (1.0 / (count * full))

    def shift(m, carry):
        own = spec_in.at[m, lat]
        pltpu.make_async_copy(own, own, spec_own.at[m]).wait()
        for mask in lat_masks:
            peer = lat_peer(mask)
            whole_in = spec_in.at[m, peer]
            remote(whole_in, whole_in, spec_send.at[m], spec_recv.at[m, peer], (lat, fr)).wait_recv()

        def tile_in(t, c0):
            r = pl.multiple_of(t * 8, 8)
            for lane in range(0, width, LANES):
                lanes = pl.ds(lane, LANES)
                cells = []
                for n in range(factor):
                    at = n * LANES
                    rows = pl.ds(at % rows_in + r, 8)
                    cells.append(
                        (spec_in[m, at // rows_in, 0, rows, lanes],
                         spec_in[m, at // rows_in, 1, rows, lanes])
                    )
                for k, (re, im) in enumerate(fft_list(cells, -1.0)):
                    if k:
                        c, s = twx[0, k, pl.ds(r, 8), :], twx[1, k, pl.ds(r, 8), :]
                        re, im = re * c + im * s, im * c - re * s
                    zs[k, pl.ds(r, 8), lanes] = re
                    zs[k, pl.ds(LANES + r, 8), lanes] = im
            return c0

        lax.fori_loop(0, LANES // 8, tile_in, 0)

        angular_mean = 2.0 * math.pi * freq_step * freq_ref[m].astype(jnp.float32) * mean
        flat = angular_mean * depth_step
        place = lat * width + lax.broadcasted_iota(jnp.int32, (LANES, width), 1)
        index_y = place // LANES + factor * (place % LANES)
        signed_y = jnp.where(index_y < full // 2, index_y, index_y - full)
        wave_y = 2.0 * math.pi / (full * grid_step) * signed_y.astype(jnp.float32)
        rest = angular_mean * angular_mean - wave_y * wave_y
        row = lax.broadcasted_iota(jnp.int32, (LANES, width), 0)

        def product(k, c0):
            high, low = split(zs[k])
            y = dot(m_both[0], high) + (dot(m_both[0], low) + dot(m_both[1], high))
            index_x = k + factor * row
            signed_x = jnp.where(index_x < count // 2, index_x, index_x - count)
            wave_x = 2.0 * math.pi / (count * grid_step) * signed_x.astype(jnp.float32)
            vertical = rest - wave_x * wave_x
            size = jnp.sqrt(jnp.abs(vertical)) * depth_step
            damping = jnp.where(vertical < 0.0, jnp.exp(-size), 1.0) * (1.0 / (count * full))
            sn, cs = sin_cos(jnp.where(vertical > 0.0, size, 0.0) - flat)
            tr, ti = damping * cs, damping * sn
            re, im = y[:LANES], y[LANES:]
            z = jnp.concatenate([re * tr - im * ti, re * ti + im * tr], axis=0)
            high, low = split(z)
            zs[k] = dot(m_both[2], high) + (dot(m_both[2], low) + dot(m_both[3], high))
            return c0

        lax.fori_loop(0, factor, product, 0)

        def tile_out(t, c0):
            r = pl.multiple_of(t * 8, 8)
            for lane in range(0, width, LANES):
                lanes = pl.ds(lane, LANES)
                cells = []
                for k in range(factor):
                    re, im = zs[k, pl.ds(r, 8), lanes], zs[k, pl.ds(LANES + r, 8), lanes]
                    if k:
                        c, s = twx[0, k, pl.ds(r, 8), :], twx[1, k, pl.ds(r, 8), :]
                        re, im = re * c - im * s, im * c + re * s
                    cells.append((re, im))
                for n, (re, im) in enumerate(fft_list(cells, 1.0)):
                    at = n * LANES
                    rows = pl.ds(at % rows_in + r, 8)
                    line_out[m, at // rows_in, 0, rows, lanes] = re
                    line_out[m, at // rows_in, 1, rows, lanes] = im
            return c0

        lax.fori_loop(0, LANES // 8, tile_out, 0)

        for d in range(strips):
            for c in range(2):
                for e in range(2):
                    beside = d - 1 if e == 0 else d + 1
                    at_row = rows_in - 1 if e == 0 else 0
                    for b in range(lane_blocks):
                        if 0 <= beside < strips:
                            value = line_out[m, beside, c, pl.ds(at_row, 1), pl.ds(b * LANES, LANES)]
                        else:
                            value = jnp.zeros((1, LANES), jnp.float32)
                        at = (c * 2 + e) * lane_blocks + b
                        edge_out[m, d, pl.ds(at, 1), :] = value

        for mask in lat_masks:
            to = lat_peer(mask)
            remote(
                edge_out.at[m, to], edge_in.at[m, lat], edge_send.at[m], edge_recv.at[m], (to, fr)
            ).start()
        pltpu.make_async_copy(edge_out.at[m, lat], edge_in.at[m, lat], edge_own.at[m]).start()

        def send_lines(i, c0):
            rows = chunk_rows(i)
            for mask in lat_masks:
                to = lat_peer(mask)
                remote(
                    line_out.at[m, to, :, rows, :], line_in.at[m, lat, :, rows, :],
                    line_send.at[m], line_recv.at[m, i], (to, fr),
                ).start()
            pltpu.make_async_copy(
                line_out.at[m, lat, :, rows, :], line_in.at[m, lat, :, rows, :], line_own.at[m, i]
            ).start()
            return c0

        lax.fori_loop(0, blocks, send_lines, 0)
        return carry

    lax.fori_loop(0, members, shift, 0)

    def columns(z, rows):
        cells = []
        for k in range(factor):
            re, im = z[k, rows, pl.ds(0, LANES)], z[k, rows, pl.ds(LANES, LANES)]
            if k:
                c, s = tw_ref[0, pl.ds(k, 1), :], tw_ref[1, pl.ds(k, 1), :]
                re, im = re * c - im * s, im * c + re * s
            cells.append((re, im))
        return fft_list(cells, 1.0)

    def inverse_dot(x):
        high, low = split(x)
        return dot(high, m_inv[0]) + (dot(low, m_inv[0]) + dot(high, m_inv[1]))

    def edges(m):
        own = edge_in.at[m, lat]
        pltpu.make_async_copy(own, own, edge_own.at[m]).wait()
        some = edge_in.at[m, pl.ds(0, strips - 1)]
        remote(some, some, edge_send.at[m], edge_recv.at[m], (lat, fr)).wait_recv()
        ze[...] = jnp.zeros_like(ze)
        for k in range(factor):
            at = k * LANES
            b = (at % width) // LANES
            for c in range(2):
                for e in range(2):
                    row_at = (c * 2 + e) * lane_blocks + b
                    ze[k, pl.ds(e, 1), pl.ds(c * LANES, LANES)] = edge_in[
                        m, at // width, pl.ds(row_at, 1), :
                    ]
        y = inverse_dot(ze[...].reshape(factor * 8, 2 * LANES))
        ze[...] = y.reshape(factor, 8, 2 * LANES)
        for n, pair in enumerate(columns(ze, pl.ds(0, 8))):
            for c in range(2):
                field[c, pl.ds(7, 1), pl.ds(n * LANES, LANES)] = pair[c][0:1]
                field[c, pl.ds(8 + rows_in, 1), pl.ds(n * LANES, LANES)] = pair[c][1:2]

    def inverse_block(m, i):
        rows = chunk_rows(i)
        own = line_in.at[m, lat, :, rows, :]
        pltpu.make_async_copy(own, own, line_own.at[m, i]).wait()
        some = line_in.at[m, pl.ds(0, strips - 1), :, rows, :]
        remote(some, some, line_send.at[m], line_recv.at[m, i], (lat, fr)).wait_recv()
        parts = []
        for k in range(factor):
            at = k * LANES
            cols = pl.ds(at % width, LANES)
            parts.append(
                jnp.concatenate(
                    [line_in[m, at // width, 0, rows, cols], line_in[m, at // width, 1, rows, cols]],
                    axis=1,
                )
            )
        y = inverse_dot(jnp.concatenate(parts, axis=0))
        zc[...] = y.reshape(factor, CHUNK, 2 * LANES)

        def tile(t, c0):
            r = pl.multiple_of(t * 8, 8)
            at_field = pl.ds(pl.multiple_of(8 + i * CHUNK + t * 8, 8), 8)
            for n, pair in enumerate(columns(zc, pl.ds(r, 8))):
                for c in range(2):
                    field[c, at_field, pl.ds(n * LANES, LANES)] = pair[c]
            return c0

        lax.fori_loop(0, CHUNK // 8, tile, 0)

    column = lax.broadcasted_iota(jnp.int32, (CHUNK, full), 1)

    def stencil(m, i):
        n = m * blocks + i
        slot = n % 2
        rows = chunk_rows(i)

        @pl.when(n + 1 < members * blocks)
        def _():
            source_copy(n + 1).start()

        @pl.when(n >= 2)
        def _():
            fresh_copy(n - 2).wait()

        source_copy(n).wait()
        angular = 2.0 * math.pi * freq_step * freq_ref[m].astype(jnp.float32)
        ahead = 0.5 / (angular * mean)
        start = pl.multiple_of(i * CHUNK, CHUNK)
        centre, laplace = [], []
        for c in range(2):
            cells = field[c, pl.ds(start, CHUNK + 16), :]
            mid = cells[8 : 8 + CHUNK]
            up = pltpu.roll(cells, 1, 0)[8 : 8 + CHUNK]
            down = pltpu.roll(cells, CHUNK + 15, 0)[8 : 8 + CHUNK]
            left = jnp.where(column == 0, 0.0, pltpu.roll(mid, 1, 1))
            right = jnp.where(column == full - 1, 0.0, pltpu.roll(mid, full - 1, 1))
            centre.append(mid)
            laplace.append(up + down + left + right - 4.0 * mid)
        slow_rows = jnp.concatenate([slow[p, rows, :] for p in range(groups)], axis=1)
        gain = (ahead - 0.5 / (angular * slow_rows)) * (depth_step / (grid_step * grid_step))
        new_re = centre[0] + gain * laplace[1]
        new_im = centre[1] - gain * laplace[0]
        fresh[slot, 0] = new_re
        fresh[slot, 1] = new_im
        fresh_copy(n).start()
        term = (new_re * source[slot, 0] + new_im * source[slot, 1]) * (
            1.0 / math.sqrt(batch_total)
        )
        for p in range(groups):
            part = term[:, p * part_width : (p + 1) * part_width]

            @pl.when(m == 0)
            def _():
                terms[p, rows, :] = part

            @pl.when(m > 0)
            def _():
                terms[p, rows, :] = terms[p, rows, :] + part

        @pl.when(m == members - 1)
        def _():
            for mask in freq_masks:
                to = freq_peer(mask)
                remote(
                    terms.at[to, rows, :], terms_in.at[fr, rows, :], term_send, term_recv.at[i],
                    (lat, to),
                ).start()
            terms_in[fr, rows, :] = terms[fr, rows, :]

    def picture_block(i):
        rows = chunk_rows(i)
        some = terms_in.at[pl.ds(0, groups - 1), rows, :]
        remote(some, some, term_send, term_recv.at[i], (lat, fr)).wait_recv()
        total = terms_in[0, rows, :]
        for p in range(1, groups):
            total = total + terms_in[p, rows, :]
        picture[rows, :] = total
        pltpu.make_async_copy(picture.at[rows, :], image_hbm.at[rows, :], image_sem).start()

    def finish(n, carry):
        m, j = n // (blocks + 1), n % (blocks + 1)

        @pl.when(j == 0)
        def _():
            edges(m)

        @pl.when(j < blocks)
        def _():
            inverse_block(m, j)

        @pl.when(j > 0)
        def _():
            stencil(m, j - 1)

        @pl.when((m == members - 1) & (j > 2))
        def _():
            picture_block(j - 3)

        return carry

    lax.fori_loop(0, members * (blocks + 1), finish, 0)
    for i in range(max(blocks - 2, 0), blocks):
        picture_block(i)
    for n in range(members * blocks - 2, members * blocks):
        fresh_copy(n).wait()
    pltpu.make_async_copy(picture, image_hbm, image_sem).wait()

    some = slow.at[pl.ds(0, groups - 1)]
    remote(some, some, slow_send, slow_recv.at[0], (lat, fr)).wait_send()
    some = terms.at[pl.ds(0, groups - 1)]
    remote(some, some, term_send, term_recv.at[0], (lat, fr)).wait_send()
    some = stat_in.at[pl.ds(0, strips - 1)]
    remote(some, some, stat_send, stat_recv, (lat, fr)).wait_send()
    for m in range(members):
        some = spec_out.at[m, pl.ds(0, strips - 1)]
        remote(some, some, spec_send.at[m], spec_recv.at[m, 0], (lat, fr)).wait_send()
        some = line_out.at[m, pl.ds(0, strips - 1)]
        remote(some, some, line_send.at[m], line_recv.at[m, 0], (lat, fr)).wait_send()
        some = edge_out.at[m, pl.ds(0, strips - 1)]
        remote(some, some, edge_send.at[m], edge_recv.at[m], (lat, fr)).wait_send()


def local(wavefield, source_field, slowness, freq_index):
    _, members, rows, full = wavefield.shape
    strips, groups = lax.axis_size("lat"), lax.axis_size("freq")
    width = full // strips
    factor = full // LANES
    part_width = full // groups
    blocks = rows // CHUNK
    tw = twiddle(full)
    tw_row = jnp.asarray(tw)
    tw_x = jnp.asarray(np.ascontiguousarray(np.broadcast_to(tw[..., None], tw.shape + (LANES,))))
    right_fwd, right_inv = dft_tables(-1.0), dft_tables(1.0)
    m_fwd, m_inv = split_table(right_fwd), split_table(right_inv)
    m_both = jnp.concatenate(
        [split_table(np.ascontiguousarray(right_fwd.T)), split_table(np.ascontiguousarray(right_inv.T))]
    )
    edge_rows = max(8, 4 * width // LANES)
    anywhere = pl.BlockSpec(memory_space=pl.ANY)
    inside = pl.BlockSpec(memory_space=pltpu.VMEM)
    f32 = jnp.float32
    dma = pltpu.SemaphoreType.DMA
    return pl.pallas_call(
        functools.partial(step_kernel, batch_total=members * groups),
        in_specs=[pl.BlockSpec(memory_space=pltpu.SMEM)] + [anywhere] * 4 + [inside] * 4,
        out_specs=[anywhere, anywhere],
        out_shape=[
            jax.ShapeDtypeStruct((2, members, rows, full), f32),
            jax.ShapeDtypeStruct((rows, part_width), f32),
        ],
        scratch_shapes=[
            pltpu.VMEM((members, strips, 2, rows, width), f32),
            pltpu.VMEM((members, strips, 2, rows, width), f32),
            pltpu.VMEM((members, strips, 2, rows, width), f32),
            pltpu.VMEM((members, strips, 2, rows, width), f32),
            pltpu.VMEM((members, strips, edge_rows, LANES), f32),
            pltpu.VMEM((members, strips, edge_rows, LANES), f32),
            pltpu.VMEM((8, LANES), f32),
            pltpu.VMEM((strips, 8, LANES), f32),
            pltpu.VMEM((groups, rows, part_width), f32),
            pltpu.VMEM((groups, rows, part_width), f32),
            pltpu.VMEM((groups, rows, part_width), f32),
            pltpu.VMEM((factor, 2 * LANES, width), f32),
            pltpu.VMEM((factor, CHUNK, 2 * LANES), f32),
            pltpu.VMEM((factor, 8, 2 * LANES), f32),
            pltpu.VMEM((2, rows + 16, full), f32),
            pltpu.VMEM(tw_x.shape, f32),
            pltpu.VMEM((2, 2, CHUNK, full), f32),
            pltpu.VMEM((2, 2, CHUNK, full), f32),
            pltpu.VMEM((2, 2, CHUNK, full), f32),
            pltpu.VMEM((rows, part_width), f32),
            dma((2,)), dma((2,)), dma((2,)), dma, dma, dma,
            dma, dma((blocks,)),
            dma((members,)), dma((members, strips)), dma((members,)),
            dma((members,)), dma((members, blocks)), dma((members, blocks)),
            dma((members,)), dma((members,)), dma((members,)),
            dma, dma,
            dma, dma((blocks,)),
        ],
        compiler_params=pltpu.CompilerParams(
            collective_id=0, has_side_effects=True, vmem_limit_bytes=VMEM_BYTES
        ),
        cost_estimate=pl.CostEstimate(
            flops=13_000_000_000, bytes_accessed=26_000_000, transcendentals=0
        ),
        name="depth_step",
    )(freq_index, wavefield, source_field, slowness, tw_x, tw_row, m_fwd, m_both, m_inv)


def solution(mesh):
    return jax.shard_map(
        local,
        mesh=mesh,
        in_specs=(
            P(None, "freq", "lat", None),
            P(None, "freq", "lat", None),
            P("lat", "freq"),
            P("freq"),
        ),
        out_specs=(P(None, "freq", "lat", None), P("lat", "freq")),
        check_vma=False,
    )
```

time: 489 us -> 395 us (0.81)
  waiting for transfers between devices: 338 us -> 0 us
  Pallas kernels: 86.9 us -> 385 us
  blocking collectives: 27.9 us -> 0 us
  starting transfers between devices: 24 us -> 0 us
    all_to_all x5 -> x0, waiting for transfers between devices: 338 us -> none  [the longest x4 314 us: exchange(): return lax.all_to_all(cells, 'lat', split_axis=0, concat_axis=0, tiled=True)]
    pallas_call x6 -> x1, Pallas kernels: 86.9 us -> 385 us  [local(): pl.pallas_call(functools.partial(step_kernel, batch_total=members * group...]
    all_to_all x1 -> x0, blocking collectives: 27.9 us -> none  [local(): lax.all_to_all(terms, 'freq', split_axis=0, concat_axis=0, tiled=True)]
    all_to_all x5 -> x0, starting transfers between devices: 24 us -> none  [the longest x4 18.8 us: exchange(): return lax.all_to_all(cells, 'lat', split_axis=0, concat_axis=0, tiled=True)]
  transfers between devices with their start and end apart: 5 -> 0, of which waited for: 5 -> 0; matrix products, arithmetic and copies ran while one was open for 0% -> 0% of each run, Pallas kernels for 13% -> 0%
where the time goes in v1:
time: 395 us
  Pallas kernels  385 us (97%)
  local copies, waits for them, and re-layouts  8.74 us (2%)
    pallas_call x1, Pallas kernels, local(): pl.pallas_call(functools.partial(step_kernel, batch_total=members * group...  385 us
    unnamed x4, local copies, waits for them, and re-layouts  8.74 us

profile of v1, /device:TPU:0, one launch (start us, length us, event | category | flops | bytes accessed | tf_op | source)
XLA Modules:
  0.0 394.6 jit_solution(9911002670843141634)
XLA Ops:
  0.6 385.2 %depth_step.1 = (f32[2,2,256,2048]{3,2,1,0:T(8,128)}, f32[256,512]{1,0:T(8,128)}) custom-call(s32[2]{0:T(128)} %freq_ref.1, f32[2,2,256,2048]{3,2,1,0:T(8,128)} %wave_hbm.1, f32[2,2,256,2048]{3,2,1,0:T(8,128)} %src_hbm.1, f32[256,512]{1,0:T(8,128)} %slow_hbm.1, f32[2,16,128,128]{3,2,1,0:T(8,128)} %constant.13.clone.twx_hbm, ...), custom_call_target="tpu_custom_call" | custom-call | flops 12999999488 | bytes 26000000 | tf_op jit(solution)/shard_map/depth_step/pallas_call | solution.py:576
  385.8 0.0 copy-start
  385.8 7.9 %copy.18 = f32[2,2,256,2048]{3,2,1,0:T(8,128)} copy(f32[2,2,256,2048]{3,2,1,0:T(8,128)} %get-tuple-element.4) | data formatting | bytes 16777216
  393.8 0.0 copy-done
  393.8 0.8 copy.19
Async XLA Ops:
  385.8 8.0 %copy-start = (f32[256,512]{1,0:T(8,128)S(1)}, f32[256,512]{1,0:T(8,128)}, u32[]{:S(2)}) copy-start(f32[256,512]{1,0:T(8,128)} %get-tuple-element.5) | copy-start | bytes 1572868

commit v2 on v1

--- a/solution.py
+++ b/solution.py
@@ -13,8 +13,10 @@
 grid_step = 25.0
 freq_step = 0.0625
 LANES = 128
-CHUNK = 32
-VMEM_BYTES = 60 * 1024 * 1024
+CHUNK = 16
+PIECE = 16
+VMEM_BYTES = 52 * 1024 * 1024
+SMALL_BYTES = 4 * 1024 * 1024
 MESH = pl.DeviceIdType.MESH
 
 
@@ -101,10 +103,10 @@
 
 def step_kernel(
     freq_ref, wave_hbm, src_hbm, slow_hbm, twx_hbm, tw_ref, m_fwd, m_both, m_inv,
-    field_hbm, image_hbm,
-    spec_out, spec_in, line_out, line_in, edge_out, edge_in, stat_out, stat_in,
-    slow, terms, terms_in, zs, zc, ze, field, twx, wave, source, fresh, picture,
-    wave_sem, source_sem, fresh_sem, image_sem, twx_sem, own_sem,
+    fresh, terms_in,
+    spec_out, spec_in, line_in, edge_out, edge_in, stat_out, stat_in,
+    slow, terms, zs, zc, zp, ze, field, twx, wave, source,
+    wave_sem, source_sem, twx_sem, own_sem,
     slow_send, slow_recv, spec_send, spec_recv, spec_own, line_send, line_recv, line_own,
     edge_send, edge_recv, edge_own, stat_send, stat_recv, term_send, term_recv,
     *, batch_total,
@@ -114,7 +116,7 @@
     full = strips * width
     factor = full // LANES
     count = rows_in * strips
-    blocks = rows_in // CHUNK
+    blocks, pieces = rows_in // CHUNK, rows_in // PIECE
     lane_blocks = width // LANES
     lat, fr = lax.axis_index("lat"), lax.axis_index("freq")
     lat_masks = sorted(range(1, strips), key=lambda m: -m)
@@ -128,6 +130,9 @@
 
     def chunk_rows(i):
         return pl.ds(pl.multiple_of(i * CHUNK, CHUNK), CHUNK)
+
+    def piece_rows(i):
+        return pl.ds(pl.multiple_of(i * PIECE, PIECE), PIECE)
 
     def remote(a, b, send, recv, to):
         return pltpu.make_async_remote_copy(
@@ -141,15 +146,9 @@
         )
 
     def source_copy(n):
-        rows = chunk_rows(n % blocks)
+        rows = piece_rows(n % pieces)
         return pltpu.make_async_copy(
-            src_hbm.at[:, n // blocks, rows, :], source.at[n % 2], source_sem.at[n % 2]
-        )
-
-    def fresh_copy(n):
-        rows = chunk_rows(n % blocks)
-        return pltpu.make_async_copy(
-            fresh.at[n % 2], field_hbm.at[:, n // blocks, rows, :], fresh_sem.at[n % 2]
+            src_hbm.at[:, n // pieces, rows, :], source.at[n % 2], source_sem.at[n % 2]
         )
 
     own_slow = pltpu.make_async_copy(slow_hbm, slow.at[fr], own_sem)
@@ -316,6 +315,8 @@
             return c0
 
         lax.fori_loop(0, factor, product, 0)
+        some = spec_out.at[m, pl.ds(0, strips - 1)]
+        remote(some, some, spec_send.at[m], spec_recv.at[m, 0], (lat, fr)).wait_send()
 
         def tile_out(t, c0):
             r = pl.multiple_of(t * 8, 8)
@@ -331,8 +332,8 @@
                 for n, (re, im) in enumerate(fft_list(cells, 1.0)):
                     at = n * LANES
                     rows = pl.ds(at % rows_in + r, 8)
-                    line_out[m, at // rows_in, 0, rows, lanes] = re
-                    line_out[m, at // rows_in, 1, rows, lanes] = im
+                    spec_out[m, at // rows_in, 0, rows, lanes] = re
+                    spec_out[m, at // rows_in, 1, rows, lanes] = im
             return c0
 
         lax.fori_loop(0, LANES // 8, tile_out, 0)
@@ -344,7 +345,7 @@
                     at_row = rows_in - 1 if e == 0 else 0
                     for b in range(lane_blocks):
                         if 0 <= beside < strips:
-                            value = line_out[m, beside, c, pl.ds(at_row, 1), pl.ds(b * LANES, LANES)]
+                            value = spec_out[m, beside, c, pl.ds(at_row, 1), pl.ds(b * LANES, LANES)]
                         else:
                             value = jnp.zeros((1, LANES), jnp.float32)
                         at = (c * 2 + e) * lane_blocks + b
@@ -358,19 +359,19 @@
         pltpu.make_async_copy(edge_out.at[m, lat], edge_in.at[m, lat], edge_own.at[m]).start()
 
         def send_lines(i, c0):
-            rows = chunk_rows(i)
+            rows = piece_rows(i)
             for mask in lat_masks:
                 to = lat_peer(mask)
                 remote(
-                    line_out.at[m, to, :, rows, :], line_in.at[m, lat, :, rows, :],
+                    spec_out.at[m, to, :, rows, :], line_in.at[m, lat, :, rows, :],
                     line_send.at[m], line_recv.at[m, i], (to, fr),
                 ).start()
             pltpu.make_async_copy(
-                line_out.at[m, lat, :, rows, :], line_in.at[m, lat, :, rows, :], line_own.at[m, i]
+                spec_out.at[m, lat, :, rows, :], line_in.at[m, lat, :, rows, :], line_own.at[m, i]
             ).start()
             return c0
 
-        lax.fori_loop(0, blocks, send_lines, 0)
+        lax.fori_loop(0, pieces, send_lines, 0)
         return carry
 
     lax.fori_loop(0, members, shift, 0)
@@ -412,7 +413,7 @@
                 field[c, pl.ds(8 + rows_in, 1), pl.ds(n * LANES, LANES)] = pair[c][1:2]
 
     def inverse_block(m, i):
-        rows = chunk_rows(i)
+        rows = piece_rows(i)
         own = line_in.at[m, lat, :, rows, :]
         pltpu.make_async_copy(own, own, line_own.at[m, i]).wait()
         some = line_in.at[m, pl.ds(0, strips - 1), :, rows, :]
@@ -428,43 +429,39 @@
                 )
             )
         y = inverse_dot(jnp.concatenate(parts, axis=0))
-        zc[...] = y.reshape(factor, CHUNK, 2 * LANES)
+        zp[...] = y.reshape(factor, PIECE, 2 * LANES)
 
         def tile(t, c0):
             r = pl.multiple_of(t * 8, 8)
-            at_field = pl.ds(pl.multiple_of(8 + i * CHUNK + t * 8, 8), 8)
-            for n, pair in enumerate(columns(zc, pl.ds(r, 8))):
+            at_field = pl.ds(pl.multiple_of(8 + i * PIECE + t * 8, 8), 8)
+            for n, pair in enumerate(columns(zp, pl.ds(r, 8))):
                 for c in range(2):
                     field[c, at_field, pl.ds(n * LANES, LANES)] = pair[c]
             return c0
 
-        lax.fori_loop(0, CHUNK // 8, tile, 0)
-
-    column = lax.broadcasted_iota(jnp.int32, (CHUNK, full), 1)
+        lax.fori_loop(0, PIECE // 8, tile, 0)
+
+    column = lax.broadcasted_iota(jnp.int32, (PIECE, full), 1)
 
     def stencil(m, i):
-        n = m * blocks + i
+        n = m * pieces + i
         slot = n % 2
-        rows = chunk_rows(i)
-
-        @pl.when(n + 1 < members * blocks)
+        rows = piece_rows(i)
+
+        @pl.when(n + 1 < members * pieces)
         def _():
             source_copy(n + 1).start()
-
-        @pl.when(n >= 2)
-        def _():
-            fresh_copy(n - 2).wait()
 
         source_copy(n).wait()
         angular = 2.0 * math.pi * freq_step * freq_ref[m].astype(jnp.float32)
         ahead = 0.5 / (angular * mean)
-        start = pl.multiple_of(i * CHUNK, CHUNK)
+        start = pl.multiple_of(i * PIECE, PIECE)
         centre, laplace = [], []
         for c in range(2):
-            cells = field[c, pl.ds(start, CHUNK + 16), :]
-            mid = cells[8 : 8 + CHUNK]
-            up = pltpu.roll(cells, 1, 0)[8 : 8 + CHUNK]
-            down = pltpu.roll(cells, CHUNK + 15, 0)[8 : 8 + CHUNK]
+            cells = field[c, pl.ds(start, PIECE + 16), :]
+            mid = cells[8 : 8 + PIECE]
+            up = pltpu.roll(cells, 1, 0)[8 : 8 + PIECE]
+            down = pltpu.roll(cells, PIECE + 15, 0)[8 : 8 + PIECE]
             left = jnp.where(column == 0, 0.0, pltpu.roll(mid, 1, 1))
             right = jnp.where(column == full - 1, 0.0, pltpu.roll(mid, full - 1, 1))
             centre.append(mid)
@@ -473,9 +470,8 @@
         gain = (ahead - 0.5 / (angular * slow_rows)) * (depth_step / (grid_step * grid_step))
         new_re = centre[0] + gain * laplace[1]
         new_im = centre[1] - gain * laplace[0]
-        fresh[slot, 0] = new_re
-        fresh[slot, 1] = new_im
-        fresh_copy(n).start()
+        fresh[0, m, rows, :] = new_re
+        fresh[1, m, rows, :] = new_im
         term = (new_re * source[slot, 0] + new_im * source[slot, 1]) * (
             1.0 / math.sqrt(batch_total)
         )
@@ -495,29 +491,19 @@
             for mask in freq_masks:
                 to = freq_peer(mask)
                 remote(
-                    terms.at[to, rows, :], terms_in.at[fr, rows, :], term_send, term_recv.at[i],
+                    terms.at[to, rows, :], terms_in.at[fr, rows, :], term_send, term_recv,
                     (lat, to),
                 ).start()
             terms_in[fr, rows, :] = terms[fr, rows, :]
 
-    def picture_block(i):
-        rows = chunk_rows(i)
-        some = terms_in.at[pl.ds(0, groups - 1), rows, :]
-        remote(some, some, term_send, term_recv.at[i], (lat, fr)).wait_recv()
-        total = terms_in[0, rows, :]
-        for p in range(1, groups):
-            total = total + terms_in[p, rows, :]
-        picture[rows, :] = total
-        pltpu.make_async_copy(picture.at[rows, :], image_hbm.at[rows, :], image_sem).start()
-
     def finish(n, carry):
-        m, j = n // (blocks + 1), n % (blocks + 1)
+        m, j = n // (pieces + 1), n % (pieces + 1)
 
         @pl.when(j == 0)
         def _():
             edges(m)
 
-        @pl.when(j < blocks)
+        @pl.when(j < pieces)
         def _():
             inverse_block(m, j)
 
@@ -525,32 +511,35 @@
         def _():
             stencil(m, j - 1)
 
-        @pl.when((m == members - 1) & (j > 2))
-        def _():
-            picture_block(j - 3)
-
         return carry
 
-    lax.fori_loop(0, members * (blocks + 1), finish, 0)
-    for i in range(max(blocks - 2, 0), blocks):
-        picture_block(i)
-    for n in range(members * blocks - 2, members * blocks):
-        fresh_copy(n).wait()
-    pltpu.make_async_copy(picture, image_hbm, image_sem).wait()
-
+    lax.fori_loop(0, members * (pieces + 1), finish, 0)
     some = slow.at[pl.ds(0, groups - 1)]
     remote(some, some, slow_send, slow_recv.at[0], (lat, fr)).wait_send()
     some = terms.at[pl.ds(0, groups - 1)]
-    remote(some, some, term_send, term_recv.at[0], (lat, fr)).wait_send()
+    remote(some, some, term_send, term_recv, (lat, fr)).wait()
     some = stat_in.at[pl.ds(0, strips - 1)]
     remote(some, some, stat_send, stat_recv, (lat, fr)).wait_send()
     for m in range(members):
         some = spec_out.at[m, pl.ds(0, strips - 1)]
-        remote(some, some, spec_send.at[m], spec_recv.at[m, 0], (lat, fr)).wait_send()
-        some = line_out.at[m, pl.ds(0, strips - 1)]
         remote(some, some, line_send.at[m], line_recv.at[m, 0], (lat, fr)).wait_send()
         some = edge_out.at[m, pl.ds(0, strips - 1)]
         remote(some, some, edge_send.at[m], edge_recv.at[m], (lat, fr)).wait_send()
+
+
+def write_kernel(fresh, terms, field_hbm, image, sem):
+    copies = [
+        pltpu.make_async_copy(fresh.at[c, m], field_hbm.at[c, m], sem)
+        for c in range(fresh.shape[0])
+        for m in range(fresh.shape[1])
+    ]
+    for copy in copies:
+        copy.start()
+    total = terms[0]
+    for p in range(1, terms.shape[0]):
+        total = total + terms[p]
+    image[...] = total
+    pltpu.make_async_copy(fresh, field_hbm, sem).wait()
 
 
 def local(wavefield, source_field, slowness, freq_index):
@@ -559,7 +548,7 @@
     width = full // strips
     factor = full // LANES
     part_width = full // groups
-    blocks = rows // CHUNK
+    blocks, pieces = rows // CHUNK, rows // PIECE
     tw = twiddle(full)
     tw_row = jnp.asarray(tw)
     tw_x = jnp.asarray(np.ascontiguousarray(np.broadcast_to(tw[..., None], tw.shape + (LANES,))))
@@ -569,20 +558,20 @@
         [split_table(np.ascontiguousarray(right_fwd.T)), split_table(np.ascontiguousarray(right_inv.T))]
     )
     edge_rows = max(8, 4 * width // LANES)
+    far = pl.BlockSpec(memory_space=pltpu.HBM)
     anywhere = pl.BlockSpec(memory_space=pl.ANY)
     inside = pl.BlockSpec(memory_space=pltpu.VMEM)
     f32 = jnp.float32
     dma = pltpu.SemaphoreType.DMA
-    return pl.pallas_call(
+    fresh, terms = pl.pallas_call(
         functools.partial(step_kernel, batch_total=members * groups),
-        in_specs=[pl.BlockSpec(memory_space=pltpu.SMEM)] + [anywhere] * 4 + [inside] * 4,
-        out_specs=[anywhere, anywhere],
+        in_specs=[pl.BlockSpec(memory_space=pltpu.SMEM)] + [far] * 4 + [inside] * 4,
+        out_specs=[inside, inside],
         out_shape=[
-            jax.ShapeDtypeStruct((2, members, rows, full), f32),
-            jax.ShapeDtypeStruct((rows, part_width), f32),
+            pltpu.VMEM((2, members, rows, full), f32),
+            pltpu.VMEM((groups, rows, part_width), f32),
         ],
         scratch_shapes=[
-            pltpu.VMEM((members, strips, 2, rows, width), f32),
             pltpu.VMEM((members, strips, 2, rows, width), f32),
             pltpu.VMEM((members, strips, 2, rows, width), f32),
             pltpu.VMEM((members, strips, 2, rows, width), f32),
@@ -592,23 +581,21 @@
             pltpu.VMEM((strips, 8, LANES), f32),
             pltpu.VMEM((groups, rows, part_width), f32),
             pltpu.VMEM((groups, rows, part_width), f32),
-            pltpu.VMEM((groups, rows, part_width), f32),
             pltpu.VMEM((factor, 2 * LANES, width), f32),
             pltpu.VMEM((factor, CHUNK, 2 * LANES), f32),
+            pltpu.VMEM((factor, PIECE, 2 * LANES), f32),
             pltpu.VMEM((factor, 8, 2 * LANES), f32),
             pltpu.VMEM((2, rows + 16, full), f32),
             pltpu.VMEM(tw_x.shape, f32),
             pltpu.VMEM((2, 2, CHUNK, full), f32),
-            pltpu.VMEM((2, 2, CHUNK, full), f32),
-            pltpu.VMEM((2, 2, CHUNK, full), f32),
-            pltpu.VMEM((rows, part_width), f32),
-            dma((2,)), dma((2,)), dma((2,)), dma, dma, dma,
+            pltpu.VMEM((2, 2, PIECE, full), f32),
+            dma((2,)), dma((2,)), dma, dma,
             dma, dma((blocks,)),
             dma((members,)), dma((members, strips)), dma((members,)),
-            dma((members,)), dma((members, blocks)), dma((members, blocks)),
+            dma((members,)), dma((members, pieces)), dma((members, pieces)),
             dma((members,)), dma((members,)), dma((members,)),
             dma, dma,
-            dma, dma((blocks,)),
+            dma, dma,
         ],
         compiler_params=pltpu.CompilerParams(
             collective_id=0, has_side_effects=True, vmem_limit_bytes=VMEM_BYTES
@@ -618,6 +605,19 @@
         ),
         name="depth_step",
     )(freq_index, wavefield, source_field, slowness, tw_x, tw_row, m_fwd, m_both, m_inv)
+    return pl.pallas_call(
+        write_kernel,
+        in_specs=[inside, inside],
+        out_specs=[anywhere, inside],
+        out_shape=[
+            jax.ShapeDtypeStruct((2, members, rows, full), f32),
+            jax.ShapeDtypeStruct((rows, part_width), f32),
+        ],
+        scratch_shapes=[dma],
+        compiler_params=pltpu.CompilerParams(vmem_limit_bytes=SMALL_BYTES),
+        cost_estimate=pl.CostEstimate(flops=400_000, bytes_accessed=8_400_000, transcendentals=0),
+        name="write_out",
+    )(fresh, terms)
 
 
 def solution(mesh):

time: 395 us -> 386 us (0.977)
  local copies, waits for them, and re-layouts: 8.74 us -> 0 us
    unnamed x4 -> x0, local copies, waits for them, and re-layouts: 8.74 us -> none
    pallas_call x1, Pallas kernels: 385 us -> 381 us  [local(): pl.pallas_call(functools.partial(step_kernel, batch_total=members * group...]
    pallas_call x0 -> x1, Pallas kernels: none -> 4.13 us  [local(): pl.pallas_call(write_kernel, in_specs=[inside, inside], out_specs=[anywhe...]
where the time goes in v2:
time: 386 us; the launch traced here: 385 us
  Pallas kernels  385 us (100%)
    pallas_call x1, Pallas kernels, local(): pl.pallas_call(functools.partial(step_kernel, batch_total=members * group...  381 us

profile of v2, /device:TPU:0, one launch (start us, length us, event | category | flops | bytes accessed | tf_op | source)
XLA Modules:
  0.0 385.4 jit_solution(7207956611287932190)
XLA Ops:
  0.6 380.6 %depth_step.1 = (f32[2,2,256,2048]{3,2,1,0:T(8,128)S(1)}, f32[4,256,512]{2,1,0:T(8,128)S(1)}) custom-call(s32[2]{0:T(128)} %freq_ref.1, f32[2,2,256,2048]{3,2,1,0:T(8,128)} %wave_hbm.1, f32[2,2,256,2048]{3,2,1,0:T(8,128)} %src_hbm.1, f32[256,512]{1,0:T(8,128)} %slow_hbm.1, f32[2,16,128,128]{3,2,1,0:T(8,128)} %constant.13.clone.twx_hbm, ...), custom_call_target="tpu_custom_call" | custom-call | flops 12999999488 | bytes 26000000 | tf_op jit(solution)/shard_map/depth_step/pallas_call | solution.py:566
  381.3 4.1 %write_out.1 = (f32[2,2,256,2048]{3,2,1,0:T(8,128)}, f32[256,512]{1,0:T(8,128)}) custom-call(f32[2,2,256,2048]{3,2,1,0:T(8,128)S(1)} %get-tuple-element.4.fresh, f32[4,256,512]{2,1,0:T(8,128)S(1)} %get-tuple-element.5.terms), custom_call_target="tpu_custom_call" | custom-call | flops 400000 | bytes 8400000 | tf_op jit(solution)/shard_map/write_out/pallas_call | solution.py:608

commit v3 on v2

--- a/solution.py
+++ b/solution.py
@@ -13,8 +13,9 @@
 grid_step = 25.0
 freq_step = 0.0625
 LANES = 128
-CHUNK = 16
-PIECE = 16
+CHUNK = 8
+PIECE = 8
+AHEAD = 2
 VMEM_BYTES = 52 * 1024 * 1024
 SMALL_BYTES = 4 * 1024 * 1024
 MESH = pl.DeviceIdType.MESH
@@ -102,11 +103,12 @@
 
 
 def step_kernel(
-    freq_ref, wave_hbm, src_hbm, slow_hbm, twx_hbm, tw_ref, m_fwd, m_both, m_inv,
+    freq_ref, wave_hbm, src_hbm, slow_hbm, twx_hbm, tw_hbm, fwd_hbm, both_hbm, inv_hbm,
     fresh, terms_in,
     spec_out, spec_in, line_in, edge_out, edge_in, stat_out, stat_in,
-    slow, terms, zs, zc, zp, ze, field, twx, wave, source,
-    wave_sem, source_sem, twx_sem, own_sem,
+    slow, terms, zs, zc, zp, ze, field, wave, source,
+    twx, tw_ref, m_fwd, m_both, m_inv,
+    wave_sem, source_sem, early_sem, late_sem, own_sem,
     slow_send, slow_recv, spec_send, spec_recv, spec_own, line_send, line_recv, line_own,
     edge_send, edge_recv, edge_own, stat_send, stat_recv, term_send, term_recv,
     *, batch_total,
@@ -151,30 +153,40 @@
             src_hbm.at[:, n // pieces, rows, :], source.at[n % 2], source_sem.at[n % 2]
         )
 
-    own_slow = pltpu.make_async_copy(slow_hbm, slow.at[fr], own_sem)
-    own_slow.start()
-    wave_copy(0).start()
-    source_copy(0).start()
-    twx_copy = pltpu.make_async_copy(twx_hbm, twx, twx_sem)
-
     barrier = pltpu.get_barrier_semaphore()
     for mask in freq_masks:
         pl.semaphore_signal(barrier, inc=1, device_id=(lat, freq_peer(mask)), device_id_type=MESH)
     for mask in lat_masks:
         pl.semaphore_signal(barrier, inc=1, device_id=(lat_peer(mask), fr), device_id_type=MESH)
+
+    own_slow = pltpu.make_async_copy(slow_hbm, slow.at[fr], own_sem)
+    own_slow.start()
+    wave_copy(0).start()
+    early = [
+        pltpu.make_async_copy(a, b, early_sem.at[i])
+        for i, (a, b) in enumerate(((tw_hbm, tw_ref), (fwd_hbm, m_fwd)))
+    ]
+    late = [
+        pltpu.make_async_copy(a, b, late_sem.at[i])
+        for i, (a, b) in enumerate(((twx_hbm, twx), (both_hbm, m_both), (inv_hbm, m_inv)))
+    ]
+    for copy in early:
+        copy.start()
     pl.semaphore_wait(barrier, len(freq_masks) + len(lat_masks))
 
     def send_slow(i, carry):
         rows = chunk_rows(i)
         for mask in freq_masks:
             remote(
-                slow_hbm.at[rows, :], slow.at[fr, rows, :], slow_send, slow_recv.at[i],
+                slow.at[fr, rows, :], slow.at[fr, rows, :], slow_send, slow_recv.at[i],
                 (lat, freq_peer(mask)),
             ).start()
         return carry
 
-    lax.fori_loop(0, blocks, send_slow, 0)
     own_slow.wait()
+    lax.fori_loop(0, min(AHEAD, blocks), send_slow, 0)
+    for copy in early:
+        copy.wait()
 
     def forward(n, carry):
         m, i = n // blocks, n % blocks
@@ -183,6 +195,10 @@
         @pl.when(n + 1 < members * blocks)
         def _():
             wave_copy(n + 1).start()
+
+        @pl.when(n + AHEAD < blocks)
+        def _():
+            send_slow(n + AHEAD, 0)
 
         @pl.when(n < blocks)
         def _():
@@ -241,6 +257,7 @@
                 return sums
 
             total = lax.fori_loop(0, rows_in // 8, add, jnp.zeros((8, LANES), jnp.float32))
+            total = jnp.sum(total, axis=0, keepdims=True)
             stat_out[...] = total
             stat_in[lat] = total
             for mask in lat_masks:
@@ -252,10 +269,13 @@
 
     lax.fori_loop(0, members * blocks, forward, 0)
 
-    twx_copy.start()
+    source_copy(0).start()
+    for copy in late:
+        copy.start()
     some = stat_in.at[pl.ds(0, strips - 1)]
     remote(some, some, stat_send, stat_recv, (lat, fr)).wait_recv()
-    twx_copy.wait()
+    for copy in late:
+        copy.wait()
     mean = jnp.sum(stat_in[...]) * (1.0 / (count * full))
 
     def shift(m, carry):
@@ -527,19 +547,23 @@
         remote(some, some, edge_send.at[m], edge_recv.at[m], (lat, fr)).wait_send()
 
 
-def write_kernel(fresh, terms, field_hbm, image, sem):
-    copies = [
-        pltpu.make_async_copy(fresh.at[c, m], field_hbm.at[c, m], sem)
-        for c in range(fresh.shape[0])
-        for m in range(fresh.shape[1])
-    ]
-    for copy in copies:
-        copy.start()
+def write_kernel(fresh, terms, field_hbm, image_hbm, image, field_sem, image_sem):
+    rows = fresh.shape[2]
+    part = rows // 4
+    for r in range(0, rows, part):
+        for c in range(fresh.shape[0]):
+            for m in range(fresh.shape[1]):
+                pltpu.make_async_copy(
+                    fresh.at[c, m, pl.ds(r, part)], field_hbm.at[c, m, pl.ds(r, part)], field_sem
+                ).start()
     total = terms[0]
     for p in range(1, terms.shape[0]):
         total = total + terms[p]
     image[...] = total
-    pltpu.make_async_copy(fresh, field_hbm, sem).wait()
+    copy = pltpu.make_async_copy(image, image_hbm, image_sem)
+    copy.start()
+    copy.wait()
+    pltpu.make_async_copy(fresh, field_hbm, field_sem).wait()
 
 
 def local(wavefield, source_field, slowness, freq_index):
@@ -565,7 +589,7 @@
     dma = pltpu.SemaphoreType.DMA
     fresh, terms = pl.pallas_call(
         functools.partial(step_kernel, batch_total=members * groups),
-        in_specs=[pl.BlockSpec(memory_space=pltpu.SMEM)] + [far] * 4 + [inside] * 4,
+        in_specs=[pl.BlockSpec(memory_space=pltpu.SMEM)] + [far] * 8,
         out_specs=[inside, inside],
         out_shape=[
             pltpu.VMEM((2, members, rows, full), f32),
@@ -577,8 +601,8 @@
             pltpu.VMEM((members, strips, 2, rows, width), f32),
             pltpu.VMEM((members, strips, edge_rows, LANES), f32),
             pltpu.VMEM((members, strips, edge_rows, LANES), f32),
-            pltpu.VMEM((8, LANES), f32),
-            pltpu.VMEM((strips, 8, LANES), f32),
+            pltpu.VMEM((1, LANES), f32),
+            pltpu.VMEM((strips, 1, LANES), f32),
             pltpu.VMEM((groups, rows, part_width), f32),
             pltpu.VMEM((groups, rows, part_width), f32),
             pltpu.VMEM((factor, 2 * LANES, width), f32),
@@ -586,10 +610,14 @@
             pltpu.VMEM((factor, PIECE, 2 * LANES), f32),
             pltpu.VMEM((factor, 8, 2 * LANES), f32),
             pltpu.VMEM((2, rows + 16, full), f32),
-            pltpu.VMEM(tw_x.shape, f32),
             pltpu.VMEM((2, 2, CHUNK, full), f32),
             pltpu.VMEM((2, 2, PIECE, full), f32),
-            dma((2,)), dma((2,)), dma, dma,
+            pltpu.VMEM(tw_x.shape, f32),
+            pltpu.VMEM(tw_row.shape, f32),
+            pltpu.VMEM(m_fwd.shape, m_fwd.dtype),
+            pltpu.VMEM(m_both.shape, m_both.dtype),
+            pltpu.VMEM(m_inv.shape, m_inv.dtype),
+            dma((2,)), dma((2,)), dma((2,)), dma((3,)), dma,
             dma, dma((blocks,)),
             dma((members,)), dma((members, strips)), dma((members,)),
             dma((members,)), dma((members, pieces)), dma((members, pieces)),
@@ -608,12 +636,12 @@
     return pl.pallas_call(
         write_kernel,
         in_specs=[inside, inside],
-        out_specs=[anywhere, inside],
+        out_specs=[anywhere, anywhere],
         out_shape=[
             jax.ShapeDtypeStruct((2, members, rows, full), f32),
             jax.ShapeDtypeStruct((rows, part_width), f32),
         ],
-        scratch_shapes=[dma],
+        scratch_shapes=[pltpu.VMEM((rows, part_width), f32), dma, dma],
         compiler_params=pltpu.CompilerParams(vmem_limit_bytes=SMALL_BYTES),
         cost_estimate=pl.CostEstimate(flops=400_000, bytes_accessed=8_400_000, transcendentals=0),
         name="write_out",

time: 386 us -> 383 us (level)
  no operation moved by 1% of the time
where the time goes in v3:
time: 383 us
  Pallas kernels  382 us (100%)
    pallas_call x1, Pallas kernels, local(): pl.pallas_call(functools.partial(step_kernel, batch_total=members * group...  378 us

profile of v3, /device:TPU:0, one launch (start us, length us, event | category | flops | bytes accessed | tf_op | source)
XLA Modules:
  0.0 382.5 jit_solution(14891178456220095315)
XLA Ops:
  0.6 378.4 %depth_step.1 = (f32[2,2,256,2048]{3,2,1,0:T(8,128)S(1)}, f32[4,256,512]{2,1,0:T(8,128)S(1)}) custom-call(s32[2]{0:T(128)} %freq_ref.1, f32[2,2,256,2048]{3,2,1,0:T(8,128)} %wave_hbm.1, f32[2,2,256,2048]{3,2,1,0:T(8,128)} %src_hbm.1, f32[256,512]{1,0:T(8,128)} %slow_hbm.1, f32[2,16,128,128]{3,2,1,0:T(8,128)} %constant.13.clone.twx_hbm, ...), custom_call_target="tpu_custom_call" | custom-call | flops 12999999488 | bytes 26000000 | tf_op jit(solution)/shard_map/depth_step/pallas_call | solution.py:590
  379.1 3.5 write_out.1

commit v4 on v3

--- a/solution.py
+++ b/solution.py
@@ -110,7 +110,7 @@
     twx, tw_ref, m_fwd, m_both, m_inv,
     wave_sem, source_sem, early_sem, late_sem, own_sem,
     slow_send, slow_recv, spec_send, spec_recv, spec_own, line_send, line_recv, line_own,
-    edge_send, edge_recv, edge_own, stat_send, stat_recv, term_send, term_recv,
+    edge_send, edge_recv, edge_own, stat_send, stat_recv, term_send, term_recv, greet,
     *, batch_total,
 ):
     members, strips, rows_in, width = (spec_out.shape[i] for i in (0, 1, 3, 4))
@@ -122,7 +122,7 @@
     lane_blocks = width // LANES
     lat, fr = lax.axis_index("lat"), lax.axis_index("freq")
     lat_masks = sorted(range(1, strips), key=lambda m: -m)
-    freq_masks = list(range(1, groups))
+    freq_masks = list(range(groups - 1, 0, -1))
 
     def lat_peer(mask):
         return flipped(lat, mask, strips)
@@ -156,7 +156,8 @@
     barrier = pltpu.get_barrier_semaphore()
     for mask in freq_masks:
         pl.semaphore_signal(barrier, inc=1, device_id=(lat, freq_peer(mask)), device_id_type=MESH)
-    for mask in lat_masks:
+    lat_bits = [bit for bit in lat_masks if bit & (bit - 1) == 0]
+    for mask in lat_bits:
         pl.semaphore_signal(barrier, inc=1, device_id=(lat_peer(mask), fr), device_id_type=MESH)
 
     own_slow = pltpu.make_async_copy(slow_hbm, slow.at[fr], own_sem)
@@ -172,19 +173,26 @@
     ]
     for copy in early:
         copy.start()
-    pl.semaphore_wait(barrier, len(freq_masks) + len(lat_masks))
-
-    def send_slow(i, carry):
-        rows = chunk_rows(i)
+    pl.semaphore_wait(barrier, len(freq_masks) + len(lat_bits))
+
+    own_slow.wait()
+    spans, first = [], 0
+    while first < blocks:
+        spans.append((first, min(max(first, 1), blocks - first)))
+        first += spans[-1][1]
+    for g, (first, size) in enumerate(spans):
+        rows = pl.ds(first * CHUNK, size * CHUNK)
         for mask in freq_masks:
             remote(
-                slow.at[fr, rows, :], slow.at[fr, rows, :], slow_send, slow_recv.at[i],
+                slow.at[fr, rows, :], slow.at[fr, rows, :], slow_send, slow_recv.at[g],
                 (lat, freq_peer(mask)),
             ).start()
-        return carry
-
-    own_slow.wait()
-    lax.fori_loop(0, min(AHEAD, blocks), send_slow, 0)
+    for stage in range(len(lat_bits) - 1):
+        for mask in lat_bits:
+            pl.semaphore_signal(
+                greet.at[stage], inc=1, device_id=(lat_peer(mask), fr), device_id_type=MESH
+            )
+        pl.semaphore_wait(greet.at[stage], len(lat_bits))
     for copy in early:
         copy.wait()
 
@@ -196,14 +204,11 @@
         def _():
             wave_copy(n + 1).start()
 
-        @pl.when(n + AHEAD < blocks)
-        def _():
-            send_slow(n + AHEAD, 0)
-
-        @pl.when(n < blocks)
-        def _():
-            some = slow.at[pl.ds(0, groups - 1), rows, :]
-            remote(some, some, slow_send, slow_recv.at[i], (lat, fr)).wait_recv()
+        for g, (first, size) in enumerate(spans):
+            @pl.when(n == first)
+            def _():
+                some = slow.at[pl.ds(0, groups - 1), pl.ds(first * CHUNK, size * CHUNK), :]
+                remote(some, some, slow_send, slow_recv.at[g], (lat, fr)).wait_recv()
 
         wave_copy(n).wait()
         scale = 2.0 * math.pi * freq_step * freq_ref[m].astype(jnp.float32) * depth_step
@@ -549,7 +554,7 @@
 
 def write_kernel(fresh, terms, field_hbm, image_hbm, image, field_sem, image_sem):
     rows = fresh.shape[2]
-    part = rows // 4
+    part = rows // 16
     for r in range(0, rows, part):
         for c in range(fresh.shape[0]):
             for m in range(fresh.shape[1]):
@@ -624,6 +629,7 @@
             dma((members,)), dma((members,)), dma((members,)),
             dma, dma,
             dma, dma,
+            pltpu.SemaphoreType.REGULAR((max(strips.bit_length() - 2, 1),)),
         ],
         compiler_params=pltpu.CompilerParams(
             collective_id=0, has_side_effects=True, vmem_limit_bytes=VMEM_BYTES

time: 383 us -> 383 us (level)
  no operation moved by 1% of the time
where the time goes in v4:
time: 383 us; the launch traced here: 382 us
  Pallas kernels  382 us (100%)
    pallas_call x1, Pallas kernels, local(): pl.pallas_call(functools.partial(step_kernel, batch_total=members * group...  378 us

profile of v4, /device:TPU:0, one launch (start us, length us, event | category | flops | bytes accessed | tf_op | source)
XLA Modules:
  0.0 382.2 jit_solution(17159149499538517145)
XLA Ops:
  0.6 378.1 %depth_step.1 = (f32[2,2,256,2048]{3,2,1,0:T(8,128)S(1)}, f32[4,256,512]{2,1,0:T(8,128)S(1)}) custom-call(s32[2]{0:T(128)} %freq_ref.1, f32[2,2,256,2048]{3,2,1,0:T(8,128)} %wave_hbm.1, f32[2,2,256,2048]{3,2,1,0:T(8,128)} %src_hbm.1, f32[256,512]{1,0:T(8,128)} %slow_hbm.1, f32[2,16,128,128]{3,2,1,0:T(8,128)} %constant.13.clone.twx_hbm, ...), custom_call_target="tpu_custom_call" | custom-call | flops 12999999488 | bytes 26000000 | tf_op jit(solution)/shard_map/depth_step/pallas_call | solution.py:595
  378.7 3.4 write_out.1

commit v5 on v3

--- a/solution.py
+++ b/solution.py
@@ -103,11 +103,11 @@
 
 
 def step_kernel(
-    freq_ref, wave_hbm, src_hbm, slow_hbm, twx_hbm, tw_hbm, fwd_hbm, both_hbm, inv_hbm,
+    freq_hbm, wave_hbm, src_hbm, slow_hbm, twx_hbm, tw_hbm, fwd_hbm, both_hbm, inv_hbm,
     fresh, terms_in,
     spec_out, spec_in, line_in, edge_out, edge_in, stat_out, stat_in,
     slow, terms, zs, zc, zp, ze, field, wave, source,
-    twx, tw_ref, m_fwd, m_both, m_inv,
+    twx, tw_ref, m_fwd, m_both, m_inv, freq_ref,
     wave_sem, source_sem, early_sem, late_sem, own_sem,
     slow_send, slow_recv, spec_send, spec_recv, spec_own, line_send, line_recv, line_own,
     edge_send, edge_recv, edge_own, stat_send, stat_recv, term_send, term_recv,
@@ -164,7 +164,7 @@
     wave_copy(0).start()
     early = [
         pltpu.make_async_copy(a, b, early_sem.at[i])
-        for i, (a, b) in enumerate(((tw_hbm, tw_ref), (fwd_hbm, m_fwd)))
+        for i, (a, b) in enumerate(((tw_hbm, tw_ref), (fwd_hbm, m_fwd), (freq_hbm, freq_ref)))
     ]
     late = [
         pltpu.make_async_copy(a, b, late_sem.at[i])
@@ -589,7 +589,7 @@
     dma = pltpu.SemaphoreType.DMA
     fresh, terms = pl.pallas_call(
         functools.partial(step_kernel, batch_total=members * groups),
-        in_specs=[pl.BlockSpec(memory_space=pltpu.SMEM)] + [far] * 8,
+        in_specs=[far] * 9,
         out_specs=[inside, inside],
         out_shape=[
             pltpu.VMEM((2, members, rows, full), f32),
@@ -617,7 +617,8 @@
             pltpu.VMEM(m_fwd.shape, m_fwd.dtype),
             pltpu.VMEM(m_both.shape, m_both.dtype),
             pltpu.VMEM(m_inv.shape, m_inv.dtype),
-            dma((2,)), dma((2,)), dma((2,)), dma((3,)), dma,
+            pltpu.SMEM((members,), jnp.int32),
+            dma((2,)), dma((2,)), dma((3,)), dma((3,)), dma,
             dma, dma((blocks,)),
             dma((members,)), dma((members, strips)), dma((members,)),
             dma((members,)), dma((members, pieces)), dma((members, pieces)),

time: 383 us -> 383 us (level)
  no operation moved by 1% of the time
where the time goes in v5:
time: 383 us; the launch traced here: 382 us
  Pallas kernels  381 us (99%)
    pallas_call x1, Pallas kernels, local(): pl.pallas_call(functools.partial(step_kernel, batch_total=members * group...  378 us

profile of v5, /device:TPU:0, one launch (start us, length us, event | category | flops | bytes accessed | tf_op | source)
XLA Modules:
  0.0 381.9 jit_solution(13661320111032555996)
XLA Ops:
  0.6 377.8 %depth_step.1 = (f32[2,2,256,2048]{3,2,1,0:T(8,128)S(1)}, f32[4,256,512]{2,1,0:T(8,128)S(1)}) custom-call(s32[2]{0:T(128)} %freq_hbm.1, f32[2,2,256,2048]{3,2,1,0:T(8,128)} %wave_hbm.1, f32[2,2,256,2048]{3,2,1,0:T(8,128)} %src_hbm.1, f32[256,512]{1,0:T(8,128)} %slow_hbm.1, f32[2,16,128,128]{3,2,1,0:T(8,128)} %constant.13.clone.twx_hbm, ...), custom_call_target="tpu_custom_call" | custom-call | flops 12999999488 | bytes 26000000 | tf_op jit(solution)/shard_map/depth_step/pallas_call | solution.py:590
  378.4 3.5 write_out.1

commit v6 on v5

--- a/solution.py
+++ b/solution.py
@@ -110,7 +110,7 @@
     twx, tw_ref, m_fwd, m_both, m_inv, freq_ref,
     wave_sem, source_sem, early_sem, late_sem, own_sem,
     slow_send, slow_recv, spec_send, spec_recv, spec_own, line_send, line_recv, line_own,
-    edge_send, edge_recv, edge_own, stat_send, stat_recv, term_send, term_recv,
+    edge_send, edge_recv, edge_own, stat_send, stat_recv, term_send, term_recv, greet,
     *, batch_total,
 ):
     members, strips, rows_in, width = (spec_out.shape[i] for i in (0, 1, 3, 4))
@@ -156,7 +156,8 @@
     barrier = pltpu.get_barrier_semaphore()
     for mask in freq_masks:
         pl.semaphore_signal(barrier, inc=1, device_id=(lat, freq_peer(mask)), device_id_type=MESH)
-    for mask in lat_masks:
+    lat_bits = [bit for bit in lat_masks if bit & (bit - 1) == 0]
+    for mask in lat_bits:
         pl.semaphore_signal(barrier, inc=1, device_id=(lat_peer(mask), fr), device_id_type=MESH)
 
     own_slow = pltpu.make_async_copy(slow_hbm, slow.at[fr], own_sem)
@@ -172,7 +173,7 @@
     ]
     for copy in early:
         copy.start()
-    pl.semaphore_wait(barrier, len(freq_masks) + len(lat_masks))
+    pl.semaphore_wait(barrier, len(freq_masks) + len(lat_bits))
 
     def send_slow(i, carry):
         rows = chunk_rows(i)
@@ -185,6 +186,12 @@
 
     own_slow.wait()
     lax.fori_loop(0, min(AHEAD, blocks), send_slow, 0)
+    for stage in range(len(lat_bits) - 1):
+        for mask in lat_bits:
+            pl.semaphore_signal(
+                greet.at[stage], inc=1, device_id=(lat_peer(mask), fr), device_id_type=MESH
+            )
+        pl.semaphore_wait(greet.at[stage], len(lat_bits))
     for copy in early:
         copy.wait()
 
@@ -625,6 +632,7 @@
             dma((members,)), dma((members,)), dma((members,)),
             dma, dma,
             dma, dma,
+            pltpu.SemaphoreType.REGULAR((max(strips.bit_length() - 2, 1),)),
         ],
         compiler_params=pltpu.CompilerParams(
             collective_id=0, has_side_effects=True, vmem_limit_bytes=VMEM_BYTES

time: 383 us -> 383 us (level)
  no operation moved by 1% of the time
where the time goes in v6:
time: 383 us; the launch traced here: 382 us
  Pallas kernels  381 us (99%)
    pallas_call x1, Pallas kernels, local(): pl.pallas_call(functools.partial(step_kernel, batch_total=members * group...  378 us

profile of v6, /device:TPU:0, one launch (start us, length us, event | category | flops | bytes accessed | tf_op | source)
XLA Modules:
  0.0 381.7 jit_solution(8525871774809791043)
XLA Ops:
  0.6 377.6 %depth_step.1 = (f32[2,2,256,2048]{3,2,1,0:T(8,128)S(1)}, f32[4,256,512]{2,1,0:T(8,128)S(1)}) custom-call(s32[2]{0:T(128)} %freq_hbm.1, f32[2,2,256,2048]{3,2,1,0:T(8,128)} %wave_hbm.1, f32[2,2,256,2048]{3,2,1,0:T(8,128)} %src_hbm.1, f32[256,512]{1,0:T(8,128)} %slow_hbm.1, f32[2,16,128,128]{3,2,1,0:T(8,128)} %constant.13.clone.twx_hbm, ...), custom_call_target="tpu_custom_call" | custom-call | flops 12999999488 | bytes 26000000 | tf_op jit(solution)/shard_map/depth_step/pallas_call | solution.py:597
  378.3 3.5 write_out.1

commit v7 on v5

--- a/solution.py
+++ b/solution.py
@@ -122,7 +122,7 @@
     lane_blocks = width // LANES
     lat, fr = lax.axis_index("lat"), lax.axis_index("freq")
     lat_masks = sorted(range(1, strips), key=lambda m: -m)
-    freq_masks = list(range(1, groups))
+    freq_masks = list(range(groups - 1, 0, -1))
 
     def lat_peer(mask):
         return flipped(lat, mask, strips)

time: 383 us -> 383 us (level)
  no operation moved by 1% of the time
where the time goes in v7:
time: 383 us; the launch traced here: 382 us
  Pallas kernels  381 us (99%)
    pallas_call x1, Pallas kernels, local(): pl.pallas_call(functools.partial(step_kernel, batch_total=members * group...  378 us

profile of v7, /device:TPU:0, one launch (start us, length us, event | category | flops | bytes accessed | tf_op | source)
XLA Modules:
  0.0 382.0 jit_solution(8611563082860696270)
XLA Ops:
  0.6 377.9 %depth_step.1 = (f32[2,2,256,2048]{3,2,1,0:T(8,128)S(1)}, f32[4,256,512]{2,1,0:T(8,128)S(1)}) custom-call(s32[2]{0:T(128)} %freq_hbm.1, f32[2,2,256,2048]{3,2,1,0:T(8,128)} %wave_hbm.1, f32[2,2,256,2048]{3,2,1,0:T(8,128)} %src_hbm.1, f32[256,512]{1,0:T(8,128)} %slow_hbm.1, f32[2,16,128,128]{3,2,1,0:T(8,128)} %constant.13.clone.twx_hbm, ...), custom_call_target="tpu_custom_call" | custom-call | flops 12999999488 | bytes 26000000 | tf_op jit(solution)/shard_map/depth_step/pallas_call | solution.py:590
  378.6 3.5 write_out.1
